TPU v7x, 256 devices: a whole 4x4x8 slice. The times are simulated.
256 devices in a mesh: dp: 16 (over z_hi, y), fsdp: 16 (over x, z_lo, core).
Axes of the slice: x: 4, y: 4, z: 8 (z_hi: 4, z_lo: 2; z = z_hi * 2 + z_lo), core: 2. Of those that a mesh axis runs over, the one named last changes fastest.
Arguments:
- tokens: bfloat16 [512, 256, 768], P(('dp', 'fsdp')), may hold values from -30 to 30
- cotangent: bfloat16 [512, 256, 768], P(('dp', 'fsdp')), may hold values from -6 to 6
- live_index: int32 [512, 256], P(('dp', 'fsdp')), may hold values from 0 to 255, as said below
- live_count: int32 [512], P(('dp', 'fsdp')), may hold values from 1 to 256, as said below
- norm_gain: bfloat16 [768], P('fsdp'), may hold values from 0.099609375 to 1.8984375
- w_first: bfloat16 [768, 3072], P('fsdp'), may hold values from -0.21875 to 0.21875
- w_second: bfloat16 [3072, 768], P('fsdp'), may hold values from -0.109375 to 0.109375
Outputs:
- layer_out: bfloat16 [512, 256, 768], P(('dp', 'fsdp'))
- token_grad: bfloat16 [512, 256, 768], P(('dp', 'fsdp'))
- grad_first: float32 [768, 3072], P('fsdp')
- grad_second: float32 [3072, 768], P('fsdp')
- grad_gain: float32 [768], P('fsdp')
Inputs may be any that keep to these rules, and one draw needn't show every extreme that they name: `live_index`: row i names each of the 256 patches once; its first live_count[i] entries are the live patches, ascending. `live_count`: images are laid out 2 to a device. For two devices with the same fsdp index whose dp indices differ by 8, round each device's number of live patches (over its 2 images) up to a multiple of 128; the two rounded numbers add up to at most 768 = 768.
All inputs are finite; a program needn't handle non-finite values.
Results may differ from a plain program's by a relative error of at most 0.0055.
Values may be sent and summed in bfloat16 or wider, within the bound.
A program may use at most 128 MiB of HBM per device.

v0:
```python
import jax
import jax.numpy as jnp
from jax import lax
from jax.sharding import PartitionSpec as P

epsilon = 1e-06
root_two_pi = 0.7978845608028654
cubic = 0.044715


def gelu_value(before):
    inner = root_two_pi * (before + cubic * before * before * before)
    return 0.5 * before * (1.0 + jnp.tanh(inner))


def gelu_slope(before):
    inner = root_two_pi * (before + cubic * before * before * before)
    tangent = jnp.tanh(inner)
    return 0.5 * (1.0 + tangent) + 0.5 * before * (1.0 - tangent * tangent) * root_two_pi * (
        1.0 + 3.0 * cubic * before * before
    )


def live_rows(live_index, live_count):
    images, patches = live_index.shape
    order = jnp.arange(patches, dtype=jnp.int32)
    marks = (order[None, :] < live_count[:, None]).astype(jnp.int32)
    owners = jnp.broadcast_to(jnp.arange(images, dtype=jnp.int32)[:, None], (images, patches))
    return jnp.zeros((images, patches), jnp.int32).at[owners, live_index].set(marks) > 0


def layer_pass(token_rows, upstream, gain_full, first_full, second_full):
    values = token_rows.astype(jnp.float32)
    center = jnp.mean(values, axis=1, keepdims=True)
    spread = jnp.mean(jnp.square(values - center), axis=1, keepdims=True)
    inverse = lax.rsqrt(spread + epsilon)
    normed = (values - center) * inverse
    gain_value = gain_full.astype(jnp.float32)
    normal_rows = (normed * gain_value).astype(jnp.bfloat16)
    before = jnp.dot(normal_rows, first_full, preferred_element_type=jnp.float32)
    hidden = gelu_value(before).astype(jnp.bfloat16)
    mixed_rows = (values + jnp.dot(hidden, second_full, preferred_element_type=jnp.float32)).astype(
        jnp.bfloat16
    )
    back_hidden = lax.dot_general(
        upstream, second_full, (((1,), (1,)), ((), ())), preferred_element_type=jnp.float32
    )
    back_before = (back_hidden * gelu_slope(before)).astype(jnp.bfloat16)
    back_normal = lax.dot_general(
        back_before, first_full, (((1,), (1,)), ((), ())), preferred_element_type=jnp.float32
    )
    gain_term = jnp.sum(back_normal * normed, axis=0)
    scaled_back = back_normal * gain_value
    grad_rows = upstream.astype(jnp.float32) + inverse * (
        scaled_back
        - jnp.mean(scaled_back, axis=1, keepdims=True)
        - normed * jnp.mean(scaled_back * normed, axis=1, keepdims=True)
    )
    return (mixed_rows, grad_rows.astype(jnp.bfloat16), gain_term, normal_rows, hidden, back_before)


def body(tokens, cotangent, live_index, live_count, norm_gain, w_first, w_second):
    images, patches, width = tokens.shape
    total_rows = images * patches
    gain_full, first_full, second_full = (
        lax.all_gather(norm_gain, "fsdp", axis=0, tiled=True),
        lax.all_gather(w_first, "fsdp", axis=0, tiled=True),
        lax.all_gather(w_second, "fsdp", axis=0, tiled=True),
    )
    flat_tokens = tokens.reshape(total_rows, width)
    flat_upstream = cotangent.reshape(total_rows, width)
    flag_column = live_rows(live_index, live_count).reshape(total_rows, 1)
    work_upstream = jnp.where(flag_column, flat_upstream, jnp.zeros_like(flat_upstream))
    work_tokens = jnp.where(flag_column, flat_tokens, jnp.zeros_like(flat_tokens))
    outcome = layer_pass(work_tokens, work_upstream, gain_full, first_full, second_full)
    layer_flat = jnp.where(flag_column, outcome[0], flat_tokens)
    grad_flat = jnp.where(flag_column, outcome[1], flat_upstream)
    gain_term = outcome[2]
    normal_rows = outcome[3]
    hidden = outcome[4]
    back_before = outcome[5]
    scale = 1.0 / patches
    first_term = (
        lax.dot_general(
            normal_rows, back_before, (((0,), (0,)), ((), ())), preferred_element_type=jnp.float32
        )
        * scale
    )
    second_term = (
        lax.dot_general(
            hidden, work_upstream, (((0,), (0,)), ((), ())), preferred_element_type=jnp.float32
        )
        * scale
    )
    gain_share, first_share, second_share = (
        lax.psum_scatter(gain_term * scale, "fsdp", scatter_dimension=0, tiled=True),
        lax.psum_scatter(first_term, "fsdp", scatter_dimension=0, tiled=True),
        lax.psum_scatter(second_term, "fsdp", scatter_dimension=0, tiled=True),
    )
    grad_gain, grad_first, grad_second = lax.psum((gain_share, first_share, second_share), "dp")
    layer_out = layer_flat.reshape(images, patches, width)
    token_grad = grad_flat.reshape(images, patches, width)
    return (layer_out, token_grad, grad_first, grad_second, grad_gain)


def solution(mesh):
    return jax.shard_map(
        body,
        mesh=mesh,
        in_specs=(
            P(("dp", "fsdp"), None, None),
            P(("dp", "fsdp"), None, None),
            P(("dp", "fsdp"), None),
            P(("dp", "fsdp")),
            P("fsdp"),
            P("fsdp", None),
            P("fsdp", None),
        ),
        out_specs=(
            P(("dp", "fsdp"), None, None),
            P(("dp", "fsdp"), None, None),
            P("fsdp", None),
            P("fsdp", None),
            P("fsdp"),
        ),
        check_vma=False,
    )
```

profile of v0, /device:TPU:1, one launch (start us, length us, event | category | flops | bytes accessed | tf_op | source)
XLA Modules:
  0.0 494.8 jit_solution(9418903870806873847)
XLA Ops:
  7.2 0.0 copy-start.3
  7.2 0.0 copy-start.4
  7.2 0.0 copy-start
  7.2 0.0 copy-start.2
  7.2 0.0 all-gather.3.cloned.1.call-start
  7.3 0.7 all-gather.3.cloned.1.call-update
  7.9 0.0 all-gather.5.cloned.1.call-start
  8.0 0.7 all-gather.5.cloned.1.call-update
  8.7 0.0 reduce-scatter.5.cloned.1.call-start
  8.8 0.7 fusion.27
  9.5 0.7 fusion.26
  10.2 24.7 %scatter_fusion = s32[2,256]{1,0:T(2,128)S(1)} fusion(s32[2,256]{1,0:T(2,128)S(1)} %broadcast.91, s32[512]{0:T(512)S(1)} %bitcast.37, s32[512]{0:T(512)S(1)} %bitcast.48), kind=kCustom, calls=%fused_computation | custom fusion | bytes 10240 | tf_op jit(solution)/shard_map/scatter | solution.py:29
  35.0 0.0 copy-done.3
  35.0 0.6 fusion.33
  36.2 0.0 copy-done.4
  36.2 0.2 dynamic-update-slice
  36.5 29.8 %all-reduce = bf16[768]{0:T(1024)(128)(2,1)S(1)} all-reduce(bf16[768]{0:T(1024)(128)(2,1)S(1)} %dynamic-update-slice), channel_id=1, replica_groups=mesh['dp'=16,'fsdp'=16] {'fsdp'}, use_global_device_ids=true, to_apply=%add | all-reduce | flops 768 | bytes 3072
  66.2 0.0 copy-done
  66.2 0.3 convert_reduce_fusion
  66.6 0.4 fusion.21
  67.0 0.0 copy-done.2
  67.1 0.3 bitcast_select_fusion
  67.3 0.0 all-gather.3.cloned.1.call-done
  67.4 4.9 fusion.31
  72.3 0.0 copy-start.5
  72.3 2.6 copy-done.5
  74.9 5.7 %convolution_multiply_fusion = f32[3072,768]{1,0:T(8,128)} fusion(bf16[512,768]{1,0:T(8,128)(2,1)S(1)} %get-tuple-element.14, f32[512,3072]{1,0:T(8,128)S(1)} %fusion.31), kind=kOutput, calls=%fused_computation.11 | convolution fusion | flops 2432434176 | bytes 16515072 | tf_op jit(solution)/shard_map/dot_general | solution.py:90
  80.6 0.0 reduce-scatter.5.cloned.1.call-update
  80.6 0.0 reduce-scatter.3.cloned.1.call-start
  80.7 17.2 %all-gather.5.cloned.1.call-done = bf16[3072,768]{1,0:T(8,128)(2,1)} async-done(((bf16[192,768]{1,0:T(8,128)(2,1)}), bf16[3072,768]{1,0:T(8,128)(2,1)}) %all-gather.5.cloned.1.call-update) | async-done | bytes 4718608 | tf_op jit(solution)/shard_map/all_gather | solution.py:68
  97.9 8.2 %fusion.6 = bf16[512,3072]{1,0:T(8,128)(2,1)S(1)} fusion(f32[512,3072]{1,0:T(8,128)} %copy-done.5, bf16[512,768]{1,0:T(8,128)(2,1)S(1)} %get-tuple-element.14, bf16[3072,768]{1,0:T(8,128)(2,1)} %all-gather.5.cloned.1.call-done), kind=kOutput, calls=%fused_computation.9 | convolution fusion | flops 2445803520 | bytes 14942208 | tf_op jit(solution)/shard_map/dot_general | solution.py:45
  106.1 0.0 copy-start.1
  106.1 1.7 copy-done.1
  107.8 5.5 %convolution_multiply_fusion.1 = f32[768,3072]{1,0:T(8,128)} fusion(bf16[512,3072]{1,0:T(8,128)(2,1)S(1)} %fusion.6, bf16[512,768]{1,0:T(8,128)(2,1)S(1)} %get-tuple-element.15, f32[768]{0:T(1024)S(1)} %convert_element_type.34, f32[512]{0:T(512)S(1)} %bitcast.45, f32[512]{0:T(512)S(1)} %bitcast.41), kind=kOutput, calls=%fused_computation.12 | convolution fusion | flops 2420244480 | bytes 13376512 | tf_op jit(solution)/shard_map/dot_general | solution.py:84
  113.3 0.0 reduce-scatter.3.cloned.1.call-update
  113.4 0.2 all-reduce.5.cloned.1.call-start
  114.2 6.3 %fusion.18 = (f32[768]{0:T(1024)S(1)}, f32[512]{0:T(512)S(1)}, f32[512]{0:T(512)S(1)}, f32[512,768]{1,0:T(8,128)S(1)}) fusion(bf16[512,768]{1,0:T(8,128)(2,1)S(1)} %get-tuple-element.15, f32[512]{0:T(512)S(1)} %bitcast.46, f32[512]{0:T(512)S(1)} %bitcast.42, f32[768]{0:T(1024)S(1)} %convert_element_type.34, bf16[512,3072]{1,0:T(8,128)(2,1)} %copy-done.1, ...), kind=kOutput, calls=%fused_computation.28 | convolution fusion | flops 2419456256 | bytes 10237952 | tf_op jit(solution)/shard_map/dot_general | solution.py:49
  120.5 1.7 fusion.23
  122.2 87.2 %reduce-scatter.5.cloned.1.call-done = f32[192,768]{1,0:T(8,128)} async-done(((f32[3072,768]{1,0:T(8,128)}), f32[192,768]{1,0:T(8,128)}) %reduce-scatter.5.cloned.1.call-update) | async-done | bytes 589840 | tf_op jit(solution)/shard_map/reduce_scatter | solution.py:98
  209.4 111.9 %reduce-scatter.3.cloned.1.call-done = f32[48,3072]{1,0:T(8,128)} async-done(((f32[768,3072]{1,0:T(8,128)}), f32[48,3072]{1,0:T(8,128)}) %reduce-scatter.3.cloned.1.call-update) | async-done | bytes 589840 | tf_op jit(solution)/shard_map/reduce_scatter | solution.py:97
  321.2 0.0 all-reduce.5.cloned.1.call-update
  321.3 29.2 %all-reduce.1 = f32[768]{0:T(1024)S(1)} all-reduce(f32[768]{0:T(1024)S(1)} %broadcast_multiply_fusion), channel_id=4, replica_groups=mesh['dp'=16,'fsdp'=16] {'fsdp'}, use_global_device_ids=true, to_apply=%region_10.11.clone | all-reduce | flops 768 | bytes 6144
  350.5 0.1 dynamic-slice.2
  350.5 39.2 %psum.23 = f32[48]{0:T(128)} all-reduce(f32[48]{0:T(128)S(1)} %dynamic-slice.2), channel_id=1, replica_groups=mesh['dp'=16,'fsdp'=16] {'dp'}, use_global_device_ids=true, to_apply=%region_11.12 | all-reduce | flops 48 | bytes 384 | tf_op jit(solution)/shard_map/psum | solution.py:100
  389.7 8.8 %fusion.22 = bf16[512,768]{1,0:T(8,128)(2,1)} fusion(bf16[512,768]{1,0:T(8,128)(2,1)S(1)} %bitcast.38, bf16[3072,768]{1,0:T(8,128)(2,1)} %all-gather.5.cloned.1.call-done, bf16[512,768]{1,0:T(8,128)(2,1)S(1)} %get-tuple-element.15, pred[512]{0:T(512)(128)(4,1)S(1)} %broadcast_in_dim.41, f32[512,3072]{1,0:T(8,128)} %copy-done.5), kind=kOutput, calls=%fused_computation.33 | convolution fusion | flops 2431647744 | bytes 13369856 | tf_op jit(solution)/shard_map/dot_general | solution.py:42
  398.6 85.8 %all-reduce.5.cloned.1.call-done = (f32[48,3072]{1,0:T(8,128)}, f32[192,768]{1,0:T(8,128)}) async-done(((f32[48,3072]{1,0:T(8,128)}, f32[192,768]{1,0:T(8,128)}), (f32[48,3072]{1,0:T(8,128)}, f32[192,768]{1,0:T(8,128)})) %all-reduce.5.cloned.1.call-update) | async-done | bytes 1179664 | tf_op jit(solution)/shard_map/psum | solution.py:100
  484.4 1.9 copy.20
  486.3 1.9 copy.21
  (13 shorter events, 0.1 us)
Async XLA Ops:
  7.2 27.8 %copy-start.3 = (u32[256]{0:T(256)S(1)}, u32[256]{0:T(256)}, u32[]{:S(2)}) copy-start(u32[256]{0:T(256)} %constant.54) | copy-start | bytes 3076
  7.2 29.1 %copy-start.4 = (bf16[48]{0:T(256)(128)(2,1)S(1)}, bf16[48]{0:T(256)(128)(2,1)}, u32[]{:S(2)}) copy-start(bf16[48]{0:T(256)(128)(2,1)} %param.11) | copy-start | bytes 292
  7.2 59.1 %copy-start = (bf16[2,256,768]{2,1,0:T(8,128)(2,1)S(1)}, bf16[2,256,768]{2,1,0:T(8,128)(2,1)}, u32[]{:S(2)}) copy-start(bf16[2,256,768]{2,1,0:T(8,128)(2,1)} %param.7) | copy-start | bytes 2359300
  7.2 59.8 %copy-start.2 = (bf16[2,256,768]{2,1,0:T(8,128)(2,1)S(1)}, bf16[2,256,768]{2,1,0:T(8,128)(2,1)}, u32[]{:S(2)}) copy-start(bf16[2,256,768]{2,1,0:T(8,128)(2,1)} %param.8) | copy-start | bytes 2359300
  7.2 60.2 %all-gather.3.cloned.1.call-start = ((), (), s32[]{:S(2)}) async-start(), calls=%async_computation.2 | async-start | bytes 5013504 | tf_op jit(solution)/shard_map/all_gather | solution.py:67
  7.9 90.0 %all-gather.5.cloned.1.call-start = ((), (), s32[]{:S(2)}) async-start(), calls=%async_computation.3 | async-start | bytes 5013504 | tf_op jit(solution)/shard_map/all_gather | solution.py:68
  8.7 200.7 %reduce-scatter.5.cloned.1.call-start = ((), (), s32[]{:S(2)}) async-start(), calls=%async_computation.5 | async-start | bytes 10027008 | tf_op jit(solution)/shard_map/reduce_scatter | solution.py:98
  72.3 2.6 copy-start.5
  80.6 240.6 %reduce-scatter.3.cloned.1.call-start = ((), (), s32[]{:S(2)}) async-start(), calls=%async_computation.4 | async-start | bytes 10027008 | tf_op jit(solution)/shard_map/reduce_scatter | solution.py:97
  106.1 1.7 copy-start.1
  113.4 371.1 %all-reduce.5.cloned.1.call-start = ((), (), s32[]{:S(2)}) async-start(), calls=%async_computation.6 | async-start | bytes 2359296 | tf_op jit(solution)/shard_map/psum | solution.py:100
Sparse Core Ops, SparseCore 0:
  9.9 45.2 all-gather.2
  57.0 40.8 all-gather.4
  100.5 108.8 reduce-scatter.4
  211.8 109.4 reduce-scatter.2
  323.8 160.5 all-reduce.4
where the time goes:
time: 504 us; the launch traced here: 495 us
  waiting for transfers between devices  304 us (60%)
  blocking collectives  98.1 us (19%)
  matrix products  39.4 us (8%)
  local copies, waits for them, and re-layouts  33.8 us (7%)
  between operations  15.3 us (3%)
    reduce_scatter x1, waiting for transfers between devices, body(): lax.psum_scatter(first_term, 'fsdp', scatter_dimension=0, tiled=True)  112 us
    reduce_scatter x1, waiting for transfers between devices, body(): lax.psum_scatter(second_term, 'fsdp', scatter_dimension=0, tiled=True)  87.2 us
    psum x1, waiting for transfers between devices, body(): lax.psum((gain_share, first_share, second_share), 'dp')  85.8 us
    unnamed x2, blocking collectives  59 us
    psum x1, blocking collectives, body(): lax.psum((gain_share, first_share, second_share), 'dp')  39.2 us
    scatter x1, local copies, waits for them, and re-layouts, live_rows(): jnp.zeros((images, patches), jnp.int32).at[owners, live_index].set(marks)  24.7 us
    all_gather x1, waiting for transfers between devices, body(): lax.all_gather(w_second, 'fsdp', axis=0, tiled=True)  17.2 us
  transfers between devices with their start and end apart: 5, of which 4 were waited for; matrix products, arithmetic and copies ran while one was open for 14% of the time, Pallas kernels for 0%

commit v1 on v0

v1 whole, which is shorter than its diff:
```python
import functools

import jax
import jax.numpy as jnp
from jax import lax
from jax.experimental import pallas as pl
from jax.experimental.pallas import tpu as pltpu
from jax.sharding import PartitionSpec as P

epsilon = 1e-06
root_two_pi = 0.7978845608028654
cubic = 0.044715

MESH = pl.DeviceIdType.MESH
NX, NY, NZH = 4, 4, 4
D, H, ROWS, PATCHES = 768, 3072, 512, 256
C = 6
HS = 192 // C
CW = 8 * HS
R1, R2 = D // 8, D * HS // CW
NB = D // CW
SR = R1 + R2
PR = SR // NY
SCALE = 1.0 / PATCHES
F32, BF16 = jnp.float32, jnp.bfloat16


def rem(a, n):
    return lax.rem(a, jnp.int32(n))


def kernel(tok, cot, idx, cnt, gain, w1, w2, o_out, o_grad, o_g1, o_g2, o_gain,
           wg, tk, ct, nrm, nt, nf, inv_s, flag_s, hid, bb, buf, r1, s1, r2, s2, r3, r4, fin, gx,
           po, pb, px, rx, gt, gsum, gz, gxx, gyy, gzz,
           ag_s, ag_r, q1_s, q1_r, q2_s, q2_r, q3_s, q3_r, q4_s, q4_r, q5_s, q5_r, q6_s, q6_r,
           w_s, w_r, l_s, t_s, t_r, gg_s, gg_r, p_s, p_r, a_s, a_r):
    dp, f = lax.axis_index("dp"), lax.axis_index("fsdp")
    x, zl, k = lax.div(f, jnp.int32(4)), rem(lax.div(f, jnp.int32(2)), 2), rem(f, 2)
    zh, y = lax.div(dp, jnp.int32(4)), rem(dp, 4)
    z, q = zh * 2 + zl, lax.div(f, jnp.int32(2))

    def dev(x_, y_, z_, k_):
        return (lax.div(z_, jnp.int32(2)) * 4 + y_, x_ * 4 + rem(z_, 2) * 2 + k_)

    z_near = zh * 2 + (1 - zl)
    z_far = rem(z + 8 + 2 * zl - 1, 8)
    partner = dev(x, y, z, 1 - k)
    near, far = dev(x, y, z_near, k), dev(x, y, z_far, k)
    xp = [dev(rem(x + i, NX), y, z, k) for i in range(1, NX)]
    yp = [dev(x, rem(y + i, NY), z, k) for i in range(1, NY)]
    zp = [dev(x, y, rem(z + 2 * i, 8), k) for i in range(1, NZH)]

    def send(src, dst, s_sem, r_sem, to):
        copy = pltpu.make_async_remote_copy(
            src_ref=src, dst_ref=dst, send_sem=s_sem, recv_sem=r_sem, device_id=to, device_id_type=MESH
        )
        copy.start()

    def got(ref, sem):
        pltpu.make_async_copy(ref, ref, sem).wait()

    everyone = [partner, near, far] + xp + yp + zp
    barrier = pltpu.get_barrier_semaphore()
    for peer in everyone:
        pl.semaphore_signal(barrier, inc=1, device_id=peer, device_id_type=MESH)
    pl.semaphore_wait(barrier, len(everyone))

    mine = pl.ds(pl.multiple_of(R1 // 2 * k, 16), R1 // 2)
    other = pl.ds(pl.multiple_of(R1 // 2 * (1 - k), 16), R1 // 2)
    send(w1.at[1 - k], wg.at[:, q, mine, :], w_s, w_r, partner)
    own = pltpu.make_async_copy(w1.at[k], wg.at[:, q, mine, :], l_s)
    own.start()
    g_own = gain[...]
    g_own = jnp.where(k == 1, pltpu.roll(g_own, 48, 1), g_own)
    gsum[0] = g_own
    send(gsum.at[0], gsum.at[1], gg_s.at[0], gg_r.at[0], partner)
    for c in range(C):
        for n in range(NB):
            wg[c, q, R1 + HS * n : R1 + HS * (n + 1), :] = w2[HS * c : HS * (c + 1), CW * n : CW * (n + 1)]
    own.wait()
    got(wg.at[:, q, other, :], w_r)

    def first_sends(c, carry):
        for i in range(1, NX):
            send(wg.at[c, q], wg.at[c, q], ag_s.at[c, i - 1], ag_r.at[c, i - 1], xp[i - 1])
        to = tuple(jnp.where(x < 2, a, b) for a, b in zip(near, far))
        send(wg.at[c, q], wg.at[c, q], ag_s.at[c, 3], ag_r.at[c, 3 + x], to)
        return carry

    lax.fori_loop(0, C, first_sends, 0)

    got(gsum.at[1], gg_r.at[0])
    gt[zl, x] = gsum[0] + gsum[1]
    for i in range(1, NX):
        send(gt.at[zl, x], gt.at[zl, x], gg_s.at[i], gg_r.at[i], xp[i - 1])

    for image in range(2):
        at = lax.broadcasted_iota(jnp.int32, (PATCHES, PATCHES), 0)
        place = lax.broadcasted_iota(jnp.int32, (PATCHES, PATCHES), 1)
        hit = jnp.where(
            jnp.logical_and(idx[image : image + 1, :] == at, place < cnt[image]), 1.0, 0.0
        ).astype(F32)
        flag = jnp.max(hit, axis=1, keepdims=True)
        rows = slice(PATCHES * image, PATCHES * (image + 1))
        flag_s[rows, :] = jnp.broadcast_to(flag, (PATCHES, 128))
        to = pl.ds(pl.multiple_of(ROWS * k + PATCHES * image, PATCHES), PATCHES)
        tk[to, :] = jnp.where(flag > 0, tok[rows, :].astype(F32), 0.0).astype(BF16)
        ct[to, :] = jnp.where(flag > 0, cot[rows, :].astype(F32), 0.0).astype(BF16)
    here = pl.ds(pl.multiple_of(ROWS * k, ROWS), ROWS)
    there = pl.ds(pl.multiple_of(ROWS * (1 - k), ROWS), ROWS)
    send(tk.at[here], tk.at[here], t_s.at[0], t_r.at[0], partner)
    send(ct.at[here], ct.at[here], t_s.at[1], t_r.at[1], partner)

    def forward(c):
        for i in range(1, NX):
            xs = rem(x + NX - i, NX)
            qs = xs * 2 + zl
            got(wg.at[c, qs], ag_r.at[c, i - 1])
            to = tuple(jnp.where(xs < 2, a, b) for a, b in zip(near, far))
            send(wg.at[c, qs], wg.at[c, qs], ag_s.at[c, 3 + i], ag_r.at[c, 3 + xs], to)

    for i in range(1, NX):
        got(gt.at[zl, rem(x + NX - i, NX)], gg_r.at[i])
    send(gt.at[zl], gt.at[zl], gg_s.at[4], gg_r.at[4], near)
    forward(0)
    got(gt.at[1 - zl], gg_r.at[4])
    got(tk.at[there], t_r.at[0])
    got(ct.at[there], t_r.at[1])

    def gain_row():
        total = jnp.zeros((8, D), F32)
        for qs in range(8):
            tile = jnp.concatenate([gt[qs % 2, qs // 2], jnp.zeros((8, D - 128), F32)], axis=1)
            total = total + (pltpu.roll(tile, 96 * qs, 1) if qs else tile)
        return total[0:1, :]

    gains = gain_row()

    def norm_step(m, carry):
        rows = pl.ds(pl.multiple_of(256 * m, 256), 256)
        values = tk[rows, :].astype(F32)
        center = jnp.mean(values, axis=1, keepdims=True)
        values = values - center
        spread = jnp.mean(values * values, axis=1, keepdims=True)
        inverse = lax.rsqrt(spread + epsilon)
        normed = values * inverse
        nf[rows, :] = normed
        inv_s[rows, :] = jnp.broadcast_to(inverse, (256, 128))
        normal = normed * gains
        nrm[rows, :] = normal.astype(BF16)
        nt[:, rows] = jnp.transpose(normal).astype(BF16)
        return carry

    lax.fori_loop(0, 4, norm_step, 0)

    def first_of(c):
        return wg[c, :, 0:R1, :].reshape(D, CW)

    def second_of(c, n):
        return wg[c, :, R1 + HS * n : R1 + HS * (n + 1), :].reshape(CW, CW)

    def grads(c):
        for i in range(4):
            qs = 2 * i + 1 - zl
            got(wg.at[c, qs], ag_r.at[c, 3 + i])

        def step(m, carry):
            rows = pl.ds(pl.multiple_of(256 * m, 256), 256)
            before = jnp.dot(nrm[rows, :], first_of(c), preferred_element_type=F32)
            back = jnp.zeros((256, CW), F32)
            for n in range(NB):
                back = back + lax.dot_general(
                    ct[rows, CW * n : CW * (n + 1)], second_of(c, n), (((1,), (1,)), ((), ())),
                    preferred_element_type=F32,
                )
            square = before * before
            tangent = jnp.tanh(before * (root_two_pi + (root_two_pi * cubic) * square))
            half = 0.5 + 0.5 * tangent
            hid[c, rows, :] = (before * half).astype(BF16)
            slope = half + (0.5 * before) * (1.0 - tangent * tangent) * (
                root_two_pi + (3.0 * cubic * root_two_pi) * square
            )
            bb[c, rows, :] = (back * slope).astype(BF16)
            return carry

        lax.fori_loop(0, 4, step, 0)
        for part in range(2):
            term = jnp.dot(nt[384 * part : 384 * (part + 1), :], bb[c], preferred_element_type=F32)
            term = (term * SCALE).astype(BF16)
            for i in range(4):
                qs = 4 * part + i
                buf[c, qs % 2, qs // 2, 0:R1, :] = term[R1 * i : R1 * (i + 1), :]
        for n in range(NB):
            term = lax.dot_general(
                hid[c], ct[:, CW * n : CW * (n + 1)], (((0,), (0,)), ((), ())), preferred_element_type=F32
            )
            term = (term * SCALE).astype(BF16)
            for qs in range(8):
                buf[c, qs % 2, qs // 2, R1 + HS * n : R1 + HS * (n + 1), :] = term[HS * qs : HS * (qs + 1), :]
        send(buf.at[c, 1 - zl, 0:2], r1.at[c, 0:2], q1_s.at[c, 0], q1_r.at[c, 0], near)
        send(buf.at[c, 1 - zl, 2:4], r1.at[c, 2:4], q1_s.at[c, 1], q1_r.at[c, 1], far)

    def along_z_lo(c):
        got(r1.at[c, 0:2], q1_r.at[c, 0])
        got(r1.at[c, 2:4], q1_r.at[c, 1])
        for i in range(NX):
            s1[c, i] = (buf[c, zl, i].astype(F32) + r1[c, i].astype(F32)).astype(BF16)
        for i in range(1, NX):
            send(s1.at[c, rem(x + i, NX)], r2.at[c, i - 1], q2_s.at[c, i - 1], q2_r.at[c, i - 1], xp[i - 1])

    def along_x(c):
        for i in range(NX - 1):
            got(r2.at[c, i], q2_r.at[c, i])
        total = s1[c, x].astype(F32)
        for i in range(NX - 1):
            total = total + r2[c, i].astype(F32)
        s2[c] = total.astype(BF16)
        for i in range(1, NY):
            part = pl.ds(pl.multiple_of(PR * rem(y + i, NY), 16), PR)
            send(s2.at[c, part], r3.at[c, i - 1], q3_s.at[c, i - 1], q3_r.at[c, i - 1], yp[i - 1])

    def along_y(c):
        for i in range(NY - 1):
            got(r3.at[c, i], q3_r.at[c, i])
        total = s2[c, pl.ds(pl.multiple_of(PR * y, 16), PR), :].astype(F32)
        for i in range(NY - 1):
            total = total + r3[c, i].astype(F32)
        r4[c, zh] = total.astype(BF16)
        for i in range(1, NZH):
            send(r4.at[c, zh], r4.at[c, zh], q4_s.at[c, i - 1], q4_r.at[c, i - 1], zp[i - 1])

    def along_z_hi(c):
        for i in range(1, NZH):
            got(r4.at[c, rem(zh + NZH - i, NZH)], q4_r.at[c, i - 1])
        total = r4[c, 0].astype(F32)
        for i in range(1, NZH):
            total = total + r4[c, i].astype(F32)
        fin[c, y] = total.astype(BF16)
        for i in range(1, NY):
            send(fin.at[c, y], fin.at[c, y], q5_s.at[c, i - 1], q5_r.at[c, i - 1], yp[i - 1])

    def back_y(c):
        for i in range(1, NY):
            got(fin.at[c, rem(y + NY - i, NY)], q5_r.at[c, i - 1])
        send(fin.at[c, 1 - k], gx.at[c], q6_s.at[c], q6_r.at[c], partner)
        o_g1[k, c] = fin[c, k]
        second = fin[c, 2:4].reshape(R2, CW)
        rows = pl.ds(pl.multiple_of(HS * c, HS), HS)
        for n in range(NB):
            o_g2[rows, CW * n : CW * (n + 1)] = second[HS * n : HS * (n + 1), :]

    def out_rows(start):
        rows = pl.ds(pl.multiple_of(start, 256), 256)
        parts = []
        for n in range(NB):
            total = jnp.zeros((256, CW), F32)
            for c in range(C):
                total = total + jnp.dot(hid[c, rows, :], second_of(c, n), preferred_element_type=F32)
            parts.append(total)
        return parts

    def back_rows(start):
        rows = pl.ds(pl.multiple_of(start, 256), 256)
        total = jnp.zeros((256, D), F32)
        for c in range(C):
            total = total + lax.dot_general(
                bb[c, rows, :], first_of(c), (((1,), (1,)), ((), ())), preferred_element_type=F32
            )
        return total

    def tail_out():
        def step(m, carry):
            rows = pl.ds(pl.multiple_of(256 * m, 256), 256)
            for n, part in enumerate(out_rows(ROWS * (1 - k) + 256 * m)):
                px[0, rows, CW * n : CW * (n + 1)] = part.astype(BF16)
            px[1, rows, :] = back_rows(ROWS * (1 - k) + 256 * m).astype(BF16)
            return carry

        lax.fori_loop(0, 2, step, 0)
        for i in range(2):
            send(px.at[i], rx.at[i], p_s.at[i], p_r.at[i], partner)

        def step(m, carry):
            rows = pl.ds(pl.multiple_of(256 * m, 256), 256)
            for n, part in enumerate(out_rows(ROWS * k + 256 * m)):
                po[rows, CW * n : CW * (n + 1)] = part
            pb[rows, :] = back_rows(ROWS * k + 256 * m)
            return carry

        lax.fori_loop(0, 2, step, 0)

    def tail_rows():
        for i in range(2):
            got(rx.at[i], p_r.at[i])
        gsum[2] = jnp.zeros((8, 128), F32)
        gsum[3] = jnp.zeros((8, 128), F32)

        def step(m, term):
            rows = pl.ds(pl.multiple_of(128 * m, 128), 128)
            at = pl.ds(pl.multiple_of(ROWS * k + 128 * m, 128), 128)
            live = flag_s[rows, :][:, 0:1] > 0
            plain = tok[rows, :].astype(F32)
            mixed = plain + (po[rows, :] + rx[0, rows, :].astype(F32))
            o_out[rows, :] = jnp.where(live, mixed, plain).astype(BF16)
            normed = nf[at, :]
            inverse = inv_s[at, :][:, 0:1]
            back = pb[rows, :] + rx[1, rows, :].astype(F32)
            product = back * normed
            scaled = back * gains
            first = jnp.mean(scaled, axis=1, keepdims=True)
            second = jnp.mean(scaled * normed, axis=1, keepdims=True)
            upstream = cot[rows, :].astype(F32)
            value = upstream + inverse * (scaled - first - normed * second)
            o_grad[rows, :] = jnp.where(live, value, upstream).astype(BF16)
            return term + jnp.sum(product.reshape(16, 8, D), axis=0)

        term = lax.fori_loop(0, 4, step, jnp.zeros((8, D), F32))
        row = jnp.broadcast_to(jnp.sum(term, axis=0, keepdims=True) * SCALE, (8, D))
        tile = jnp.zeros((8, 128), F32)
        line = lax.broadcasted_iota(jnp.int32, (8, 128), 0)
        lane = lax.broadcasted_iota(jnp.int32, (8, 128), 1)
        for qs in range(8):
            turned = (pltpu.roll(row, D - 96 * qs, 1) if qs else row)[:, 0:128]
            tile = jnp.where(jnp.logical_and(line == qs, lane < 96), turned, tile)
        gz[0] = tile
        send(gz.at[0], gz.at[1], a_s.at[0], a_r.at[0], partner)

    def gain_z_lo():
        got(gz.at[1], a_r.at[0])
        gz[2] = gz[0] + gz[1]
        send(gz.at[2], gz.at[3], a_s.at[1], a_r.at[1], near)

    def gain_x():
        got(gz.at[3], a_r.at[1])
        gxx[x] = gz[2] + gz[3]
        for i in range(1, NX):
            send(gxx.at[x], gxx.at[x], a_s.at[1 + i], a_r.at[1 + i], xp[i - 1])

    def gain_y():
        for i in range(1, NX):
            got(gxx.at[rem(x + NX - i, NX)], a_r.at[1 + i])
        gyy[y] = gxx[0] + gxx[1] + gxx[2] + gxx[3]
        for i in range(1, NY):
            send(gyy.at[y], gyy.at[y], a_s.at[4 + i], a_r.at[4 + i], yp[i - 1])

    def gain_z_hi():
        for i in range(1, NY):
            got(gyy.at[rem(y + NY - i, NY)], a_r.at[4 + i])
        gzz[zh] = gyy[0] + gyy[1] + gyy[2] + gyy[3]
        for i in range(1, NZH):
            send(gzz.at[zh], gzz.at[zh], a_s.at[7 + i], a_r.at[7 + i], zp[i - 1])

    def gain_last():
        for i in range(1, NZH):
            got(gzz.at[rem(zh + NZH - i, NZH)], a_r.at[7 + i])
        o_gain[...] = gzz[0] + gzz[1] + gzz[2] + gzz[3]

    def slot(t, carry):
        @pl.when(t + 1 < C)
        def _():
            forward(t + 1)

        @pl.when(t < C)
        def _():
            grads(t)

        @pl.when(t == C)
        def _():
            tail_out()

        @pl.when(t == C + 1)
        def _():
            tail_rows()

        for late, work in ((1, along_z_lo), (2, along_x), (3, along_y), (4, along_z_hi), (5, back_y)):

            @pl.when(jnp.logical_and(t >= late, t < C + late))
            def _():
                work(t - late)

        return carry

    lax.fori_loop(0, C + 2, slot, 0)
    gain_z_lo()
    along_y(C - 1)
    along_z_hi(C - 2)
    back_y(C - 3)
    gain_x()
    along_z_hi(C - 1)
    gain_y()
    back_y(C - 2)
    gain_z_hi()
    back_y(C - 1)
    gain_last()

    def last(c, carry):
        got(gx.at[c], q6_r.at[c])
        o_g1[1 - k, c] = gx[c]
        for i in range(4):
            got(wg.at[c, q], ag_s.at[c, i])
        for i in range(1, NX):
            got(wg.at[c, q], ag_s.at[c, 3 + i])
        got(r1.at[c, 0:2], q1_s.at[c, 0])
        got(r1.at[c, 2:4], q1_s.at[c, 1])
        for i in range(3):
            got(r2.at[c, i], q2_s.at[c, i])
            got(r3.at[c, i], q3_s.at[c, i])
            got(r4.at[c, zh], q4_s.at[c, i])
            got(fin.at[c, y], q5_s.at[c, i])
        got(gx.at[c], q6_s.at[c])
        return carry

    lax.fori_loop(0, C, last, 0)
    got(wg.at[:, q, mine, :], w_s)
    for i in range(2):
        got(tk.at[here], t_s.at[i])
        got(px.at[i], p_s.at[i])
    for i in range(4):
        got(gsum.at[0], gg_s.at[i])
    got(gt.at[zl], gg_s.at[4])
    for i in range(11):
        got(gz.at[0], a_s.at[i])


def body(tokens, cotangent, live_index, live_count, norm_gain, w_first, w_second):
    images, patches, width = tokens.shape
    tok, cot = tokens.reshape(ROWS, D), cotangent.reshape(ROWS, D)
    gain = jnp.broadcast_to(jnp.pad(norm_gain.astype(F32), (0, 80))[None], (8, 128))
    w1 = w_first.reshape(48, 8, 2, C, HS).transpose(2, 3, 0, 1, 4).reshape(2, C, 48, CW)
    vmem = pl.BlockSpec(memory_space=pltpu.VMEM)
    smem = pl.BlockSpec(memory_space=pltpu.SMEM)
    dma = pltpu.SemaphoreType.DMA
    scratch = [
        pltpu.VMEM((C, 8, SR, CW), BF16),
        pltpu.VMEM((2 * ROWS, D), BF16),
        pltpu.VMEM((2 * ROWS, D), BF16),
        pltpu.VMEM((2 * ROWS, D), BF16),
        pltpu.VMEM((D, 2 * ROWS), BF16),
        pltpu.VMEM((2 * ROWS, D), F32),
        pltpu.VMEM((2 * ROWS, 128), F32),
        pltpu.VMEM((ROWS, 128), F32),
        pltpu.VMEM((C, 2 * ROWS, CW), BF16),
        pltpu.VMEM((C, 2 * ROWS, CW), BF16),
        pltpu.VMEM((C, 2, NX, SR, CW), BF16),
        pltpu.VMEM((C, NX, SR, CW), BF16),
        pltpu.VMEM((C, NX, SR, CW), BF16),
        pltpu.VMEM((C, NX - 1, SR, CW), BF16),
        pltpu.VMEM((C, SR, CW), BF16),
        pltpu.VMEM((C, NY - 1, PR, CW), BF16),
        pltpu.VMEM((C, NZH, PR, CW), BF16),
        pltpu.VMEM((C, NY, PR, CW), BF16),
        pltpu.VMEM((C, PR, CW), BF16),
        pltpu.VMEM((ROWS, D), F32),
        pltpu.VMEM((ROWS, D), F32),
        pltpu.VMEM((2, ROWS, D), BF16),
        pltpu.VMEM((2, ROWS, D), BF16),
        pltpu.VMEM((2, NX, 8, 128), F32),
        pltpu.VMEM((4, 8, 128), F32),
        pltpu.VMEM((4, 8, 128), F32),
        pltpu.VMEM((4, 8, 128), F32),
        pltpu.VMEM((4, 8, 128), F32),
        pltpu.VMEM((4, 8, 128), F32),
        dma((C, 7)), dma((C, 7)),
        dma((C, 2)), dma((C, 2)),
        dma((C, 3)), dma((C, 3)),
        dma((C, 3)), dma((C, 3)),
        dma((C, 3)), dma((C, 3)),
        dma((C, 3)), dma((C, 3)),
        dma((C,)), dma((C,)),
        dma, dma, dma,
        dma((2,)), dma((2,)),
        dma((5,)), dma((5,)),
        dma((2,)), dma((2,)),
        dma((11,)), dma((11,)),
    ]
    out, grad, g1, g2, gg = pl.pallas_call(
        kernel,
        out_shape=(
            jax.ShapeDtypeStruct((ROWS, D), BF16),
            jax.ShapeDtypeStruct((ROWS, D), BF16),
            jax.ShapeDtypeStruct((2, C, 48, CW), BF16),
            jax.ShapeDtypeStruct((192, D), BF16),
            jax.ShapeDtypeStruct((8, 128), F32),
        ),
        in_specs=[vmem, vmem, vmem, smem, vmem, vmem, vmem],
        out_specs=(vmem,) * 5,
        scratch_shapes=scratch,
        compiler_params=pltpu.CompilerParams(
            collective_id=0, has_side_effects=True, vmem_limit_bytes=60 << 20
        ),
        cost_estimate=pl.CostEstimate(flops=14 * 10**9, bytes_accessed=10**7, transcendentals=0),
    )(tok, cot, live_index, live_count, gain, w1, w_second)
    f = lax.axis_index("fsdp")
    grad_first = g1.reshape(2, C, 48, 8, HS).transpose(2, 3, 0, 1, 4).reshape(48, H).astype(F32)
    grad_gain = lax.dynamic_slice(gg, (f // 2, 48 * (f % 2)), (1, 48)).reshape(48)
    return (
        out.reshape(images, patches, width),
        grad.reshape(images, patches, width),
        grad_first,
        g2.astype(F32),
        grad_gain,
    )


def solution(mesh):
    return jax.shard_map(
        body,
        mesh=mesh,
        in_specs=(
            P(("dp", "fsdp"), None, None),
            P(("dp", "fsdp"), None, None),
            P(("dp", "fsdp"), None),
            P(("dp", "fsdp")),
            P("fsdp"),
            P("fsdp", None),
            P("fsdp", None),
        ),
        out_specs=(
            P(("dp", "fsdp"), None, None),
            P(("dp", "fsdp"), None, None),
            P("fsdp", None),
            P("fsdp", None),
            P("fsdp"),
        ),
        check_vma=False,
    )
```

time: 504 us -> 143 us (0.28); the launches traced: 495 us -> 142 us
  waiting for transfers between devices: 304 us -> 0 us
  Pallas kernels: 0 us -> 127 us
  blocking collectives: 98.1 us -> 0 us
  matrix products: 39.4 us -> 0 us
  local copies, waits for them, and re-layouts: 33.8 us -> 13.6 us
  between operations: 15.3 us -> 0.71 us
    reduce_scatter x2 -> x0, waiting for transfers between devices: 199 us -> none  [the longest x1 112 us: body(): lax.psum_scatter(first_term, 'fsdp', scatter_dimension=0, tiled=True)]
    pallas_call x0 -> x1, Pallas kernels: none -> 127 us  [body(): pl.pallas_call(kernel, out_shape=(jax.ShapeDtypeStruct((ROWS, D), BF16),...]
    psum x1 -> x0, waiting for transfers between devices: 85.8 us -> none  [body(): lax.psum((gain_share, first_share, second_share), 'dp')]
    unnamed x2 -> x0, blocking collectives: 59 us -> none
    dot_general x6 -> x0, matrix products: 39.4 us -> none  [the longest x1 8.85 us: layer_pass(): jnp.dot(hidden, second_full, preferred_element_type=jnp.float32)]
    psum x1 -> x0, blocking collectives: 39.2 us -> none  [body(): lax.psum((gain_share, first_share, second_share), 'dp')]
    scatter x1 -> x0, local copies, waits for them, and re-layouts: 24.7 us -> none  [live_rows(): jnp.zeros((images, patches), jnp.int32).at[owners, live_index].set(marks)]
    all_gather x2 -> x0, waiting for transfers between devices: 17.3 us -> none  [the longest x1 17.2 us: body(): lax.all_gather(w_second, 'fsdp', axis=0, tiled=True)]
  transfers between devices with their start and end apart: 5 -> 0, of which waited for: 4 -> 0; matrix products, arithmetic and copies ran while one was open for 14% -> 0% of each run, Pallas kernels for 0% -> 0%
where the time goes in v1:
time: 143 us; the launch traced here: 142 us
  Pallas kernels  127 us (89%)
  local copies, waits for them, and re-layouts  13.6 us (10%)
    pallas_call x1, Pallas kernels, body(): pl.pallas_call(kernel, out_shape=(jax.ShapeDtypeStruct((ROWS, D), BF16),...  127 us
    unnamed x12, local copies, waits for them, and re-layouts  5.87 us
    convert_element_type x2, local copies, waits for them, and re-layouts, body(): g1.reshape(2, C, 48, 8, HS).transpose(2, 3, 0, 1, 4).reshape(48, H)  3.46 us

profile of v1, /device:TPU:1, one launch (start us, length us, event | category | flops | bytes accessed | tf_op | source)
XLA Modules:
  0.0 142.2 jit_solution(11827277204379384185)
XLA Ops:
  0.7 1.3 copy.14
  2.0 0.0 copy-start.3
  2.0 0.8 copy.15
  2.9 1.5 %reshape.41.w1 = bf16[2,6,48,256]{3,2,1,0:T(8,128)(2,1)} reshape(bf16[2,6,48,8,32]{4,3,2,1,0:T(8,128)(2,1)S(1)} %copy.15) | data formatting | bytes 589824 | tf_op jit(solution)/shard_map/reshape | solution.py:429
  4.4 0.0 copy-done.3
  4.4 0.6 broadcast_in_dim.2.gain
  5.0 127.0 %shard_map.110 = (bf16[512,768]{1,0:T(8,128)(2,1)}, bf16[512,768]{1,0:T(8,128)(2,1)}, bf16[2,6,48,256]{3,2,1,0:T(8,128)(2,1)}, bf16[192,768]{1,0:T(8,128)(2,1)}, f32[8,128]{1,0:T(8,128)}) custom-call(bf16[512,768]{1,0:T(8,128)(2,1)} %bitcast.20, bf16[512,768]{1,0:T(8,128)(2,1)} %bitcast.21, s32[2,256]{1,0:T(2,128)} %idx.1, s32[2]{0:T(128)} %cnt.1, ...), custom_call_target="tpu_custom_call" | custom-call | flops 14000000000 | bytes 10000000 | tf_op jit(solution)/shard_map/pallas_call | solution.py:476
  132.0 1.3 dynamic-slice_bitcast_fusion
  133.3 1.6 %reshape.46 = f32[2,6,48,8,32]{4,3,2,1,0:T(8,128)S(1)} reshape(bf16[2,6,48,256]{3,2,1,0:T(8,128)(2,1)} %get-tuple-element.12) | data formatting | bytes 884736 | tf_op jit(solution)/shard_map/convert_element_type | solution.py:494
  134.9 1.9 %copy.16 = f32[48,8,2,6,32]{0,4,3,2,1:T(8,128)} copy(f32[48,8,2,6,32]{4,1,0,3,2:T(8,128)S(1)} %bitcast.15) | data formatting | bytes 1179648 | tf_op jit(solution)/shard_map/convert_element_type | solution.py:494
  136.8 0.0 copy-start.2
  136.8 0.0 copy-start.1
  136.8 2.8 %copy.17 = f32[48,3072]{1,0:T(8,128)} copy(f32[48,3072]{0,1:T(8,128)} %bitcast.16) | data formatting | bytes 1179648
  139.6 0.0 copy-start
  139.6 0.0 copy-done.2
  139.6 0.9 convert_element_type.22
  140.4 0.0 copy-done.1
  140.4 0.9 copy.20
  141.3 0.0 copy-done
  141.3 0.9 copy.21
  (1 shorter events, 0.0 us)
Async XLA Ops:
  2.0 2.4 %copy-start.3 = (bf16[48]{0:T(256)(128)(2,1)S(1)}, bf16[48]{0:T(256)(128)(2,1)}, u32[]{:S(2)}) copy-start(bf16[48]{0:T(256)(128)(2,1)} %param.11) | copy-start | bytes 292
  136.8 2.8 %copy-start.2 = (bf16[192,768]{1,0:T(8,128)(2,1)S(1)}, bf16[192,768]{1,0:T(8,128)(2,1)}, u32[]{:S(2)}) copy-start(bf16[192,768]{1,0:T(8,128)(2,1)} %get-tuple-element.13) | copy-start | bytes 884740
  136.8 3.6 %copy-start.1 = (bf16[512,768]{1,0:T(8,128)(2,1)S(1)}, bf16[512,768]{1,0:T(8,128)(2,1)}, u32[]{:S(2)}) copy-start(bf16[512,768]{1,0:T(8,128)(2,1)} %get-tuple-element.10) | copy-start | bytes 2359300
  139.6 1.7 %copy-start = (bf16[512,768]{1,0:T(8,128)(2,1)S(1)}, bf16[512,768]{1,0:T(8,128)(2,1)}, u32[]{:S(2)}) copy-start(bf16[512,768]{1,0:T(8,128)(2,1)} %get-tuple-element.11) | copy-start | bytes 2359300

commit v2 on v1

--- a/solution.py
+++ b/solution.py
@@ -14,6 +14,7 @@
 MESH = pl.DeviceIdType.MESH
 NX, NY, NZH = 4, 4, 4
 D, H, ROWS, PATCHES = 768, 3072, 512, 256
+AHEAD = 2
 C = 6
 HS = 192 // C
 CW = 8 * HS
@@ -29,9 +30,9 @@
     return lax.rem(a, jnp.int32(n))
 
 
-def kernel(tok, cot, idx, cnt, gain, w1, w2, o_out, o_grad, o_g1, o_g2, o_gain,
-           wg, tk, ct, nrm, nt, nf, inv_s, flag_s, hid, bb, buf, r1, s1, r2, s2, r3, r4, fin, gx,
-           po, pb, px, rx, gt, gsum, gz, gxx, gyy, gzz,
+def kernel(tok, cot, idx, cnt, gain, w_in, w2, o_out, o_grad, o_g1, o_g2, o_gain,
+           w1, wg, tk, ct, nrm, nt, nf, inv_s, flag_s, hid, bb, buf, r1, s1, r2, s2, r3, r4, fin, gx,
+           go, po, pb, px, rx, gt, gsum, gacc, gz, gxx, gyy, gzz,
            ag_s, ag_r, q1_s, q1_r, q2_s, q2_r, q3_s, q3_r, q4_s, q4_r, q5_s, q5_r, q6_s, q6_r,
            w_s, w_r, l_s, t_s, t_r, gg_s, gg_r, p_s, p_r, a_s, a_r):
     dp, f = lax.axis_index("dp"), lax.axis_index("fsdp")
@@ -63,6 +64,32 @@
     barrier = pltpu.get_barrier_semaphore()
     for peer in everyone:
         pl.semaphore_signal(barrier, inc=1, device_id=peer, device_id_type=MESH)
+
+    lane = lax.broadcasted_iota(jnp.int32, (R1 // 2, 128), 1)
+    per = 128 // HS
+
+    def gather_lanes(pieces):
+        block = None
+        for i, (value, at) in enumerate(pieces):
+            turned = value if at == i else pltpu.roll(value, (i - at) * HS % 128, 1)
+            block = turned if block is None else jnp.where(lane >= HS * i, turned, block)
+        return block
+
+    def hidden_block(core, c, qs):
+        return (2 * qs + core) * C + c
+
+    for core in range(2):
+        for c in range(C):
+            for part in range(CW // 128):
+                pieces = []
+                for i in range(per):
+                    block = hidden_block(core, c, per * part + i)
+                    start = block // per * 128
+                    pieces.append((w_in[:, start : start + 128].astype(F32), block % per))
+                w1[core, c, :, 128 * part : 128 * (part + 1)] = gather_lanes(pieces).astype(BF16)
+    gsum[0] = jnp.zeros((8, 128), F32)
+    gsum[0, :, 0:48] = jnp.broadcast_to(gain[...].astype(F32), (8, 48))
+    gacc[...] = jnp.zeros((8, D), F32)
     pl.semaphore_wait(barrier, len(everyone))
 
     mine = pl.ds(pl.multiple_of(R1 // 2 * k, 16), R1 // 2)
@@ -70,7 +97,7 @@
     send(w1.at[1 - k], wg.at[:, q, mine, :], w_s, w_r, partner)
     own = pltpu.make_async_copy(w1.at[k], wg.at[:, q, mine, :], l_s)
     own.start()
-    g_own = gain[...]
+    g_own = gsum[0]
     g_own = jnp.where(k == 1, pltpu.roll(g_own, 48, 1), g_own)
     gsum[0] = g_own
     send(gsum.at[0], gsum.at[1], gg_s.at[0], gg_r.at[0], partner)
@@ -87,7 +114,7 @@
         send(wg.at[c, q], wg.at[c, q], ag_s.at[c, 3], ag_r.at[c, 3 + x], to)
         return carry
 
-    lax.fori_loop(0, C, first_sends, 0)
+    lax.fori_loop(0, AHEAD, first_sends, 0)
 
     got(gsum.at[1], gg_r.at[0])
     gt[zl, x] = gsum[0] + gsum[1]
@@ -186,6 +213,17 @@
         lax.fori_loop(0, 4, step, 0)
         for part in range(2):
             term = jnp.dot(nt[384 * part : 384 * (part + 1), :], bb[c], preferred_element_type=F32)
+            own_rows = wg[c, 4 * part : 4 * (part + 1), 0:R1, :].reshape(384, CW)
+            product = term * own_rows.astype(F32)
+            high = product.astype(BF16)
+            low = (product - high.astype(F32)).astype(BF16)
+            ones = jnp.ones((8, CW), BF16)
+            line_sum = jnp.zeros((8, 384), F32)
+            for share in (high, low):
+                line_sum = line_sum + lax.dot_general(
+                    ones, share, (((1,), (1,)), ((), ())), preferred_element_type=F32
+                )
+            gacc[:, 384 * part : 384 * (part + 1)] += line_sum
             term = (term * SCALE).astype(BF16)
             for i in range(4):
                 qs = 4 * part + i
@@ -243,11 +281,11 @@
         for i in range(1, NY):
             got(fin.at[c, rem(y + NY - i, NY)], q5_r.at[c, i - 1])
         send(fin.at[c, 1 - k], gx.at[c], q6_s.at[c], q6_r.at[c], partner)
-        o_g1[k, c] = fin[c, k]
+        go[k, c] = fin[c, k].astype(F32)
         second = fin[c, 2:4].reshape(R2, CW)
         rows = pl.ds(pl.multiple_of(HS * c, HS), HS)
         for n in range(NB):
-            o_g2[rows, CW * n : CW * (n + 1)] = second[HS * n : HS * (n + 1), :]
+            o_g2[rows, CW * n : CW * (n + 1)] = second[HS * n : HS * (n + 1), :].astype(F32)
 
     def out_rows(start):
         rows = pl.ds(pl.multiple_of(start, 256), 256)
@@ -292,10 +330,8 @@
     def tail_rows():
         for i in range(2):
             got(rx.at[i], p_r.at[i])
-        gsum[2] = jnp.zeros((8, 128), F32)
-        gsum[3] = jnp.zeros((8, 128), F32)
-
-        def step(m, term):
+
+        def step(m, carry):
             rows = pl.ds(pl.multiple_of(128 * m, 128), 128)
             at = pl.ds(pl.multiple_of(ROWS * k + 128 * m, 128), 128)
             live = flag_s[rows, :][:, 0:1] > 0
@@ -305,23 +341,23 @@
             normed = nf[at, :]
             inverse = inv_s[at, :][:, 0:1]
             back = pb[rows, :] + rx[1, rows, :].astype(F32)
-            product = back * normed
             scaled = back * gains
             first = jnp.mean(scaled, axis=1, keepdims=True)
             second = jnp.mean(scaled * normed, axis=1, keepdims=True)
             upstream = cot[rows, :].astype(F32)
             value = upstream + inverse * (scaled - first - normed * second)
             o_grad[rows, :] = jnp.where(live, value, upstream).astype(BF16)
-            return term + jnp.sum(product.reshape(16, 8, D), axis=0)
-
-        term = lax.fori_loop(0, 4, step, jnp.zeros((8, D), F32))
-        row = jnp.broadcast_to(jnp.sum(term, axis=0, keepdims=True) * SCALE, (8, D))
+            return carry
+
+        lax.fori_loop(0, 4, step, 0)
+
+    def gain_core():
+        row = gacc[...] * SCALE / gains
         tile = jnp.zeros((8, 128), F32)
         line = lax.broadcasted_iota(jnp.int32, (8, 128), 0)
-        lane = lax.broadcasted_iota(jnp.int32, (8, 128), 1)
         for qs in range(8):
             turned = (pltpu.roll(row, D - 96 * qs, 1) if qs else row)[:, 0:128]
-            tile = jnp.where(jnp.logical_and(line == qs, lane < 96), turned, tile)
+            tile = jnp.where(line == qs, turned, tile)
         gz[0] = tile
         send(gz.at[0], gz.at[1], a_s.at[0], a_r.at[0], partner)
 
@@ -353,9 +389,18 @@
     def gain_last():
         for i in range(1, NZH):
             got(gzz.at[rem(zh + NZH - i, NZH)], a_r.at[7 + i])
-        o_gain[...] = gzz[0] + gzz[1] + gzz[2] + gzz[3]
+        total = gzz[0] + gzz[1] + gzz[2] + gzz[3]
+        line = lax.broadcasted_iota(jnp.int32, (8, 128), 0)
+        row = jnp.sum(jnp.where(line == q, total, 0.0), axis=0, keepdims=True)
+        row = jnp.broadcast_to(row, (8, 128))
+        row = jnp.where(k == 1, pltpu.roll(row, 80, 1), row)
+        o_gain[...] = row[0:1, 0:48]
 
     def slot(t, carry):
+        @pl.when(t + AHEAD < C)
+        def _():
+            first_sends(t + AHEAD, 0)
+
         @pl.when(t + 1 < C)
         def _():
             forward(t + 1)
@@ -366,6 +411,7 @@
 
         @pl.when(t == C)
         def _():
+            gain_core()
             tail_out()
 
         @pl.when(t == C + 1)
@@ -395,7 +441,7 @@
 
     def last(c, carry):
         got(gx.at[c], q6_r.at[c])
-        o_g1[1 - k, c] = gx[c]
+        go[1 - k, c] = gx[c].astype(F32)
         for i in range(4):
             got(wg.at[c, q], ag_s.at[c, i])
         for i in range(1, NX):
@@ -411,6 +457,18 @@
         return carry
 
     lax.fori_loop(0, C, last, 0)
+    place = {}
+    for core in range(2):
+        for c in range(C):
+            for qs in range(8):
+                place[hidden_block(core, c, qs)] = (core, c, qs)
+    for block in range(H // 128):
+        pieces = []
+        for i in range(per):
+            core, c, qs = place[per * block + i]
+            start = qs // per * 128
+            pieces.append((go[core, c, :, start : start + 128], qs % per))
+        o_g1[:, 128 * block : 128 * (block + 1)] = gather_lanes(pieces)
     got(wg.at[:, q, mine, :], w_s)
     for i in range(2):
         got(tk.at[here], t_s.at[i])
@@ -425,12 +483,11 @@
 def body(tokens, cotangent, live_index, live_count, norm_gain, w_first, w_second):
     images, patches, width = tokens.shape
     tok, cot = tokens.reshape(ROWS, D), cotangent.reshape(ROWS, D)
-    gain = jnp.broadcast_to(jnp.pad(norm_gain.astype(F32), (0, 80))[None], (8, 128))
-    w1 = w_first.reshape(48, 8, 2, C, HS).transpose(2, 3, 0, 1, 4).reshape(2, C, 48, CW)
     vmem = pl.BlockSpec(memory_space=pltpu.VMEM)
     smem = pl.BlockSpec(memory_space=pltpu.SMEM)
     dma = pltpu.SemaphoreType.DMA
     scratch = [
+        pltpu.VMEM((2, C, R1 // 2, CW), BF16),
         pltpu.VMEM((C, 8, SR, CW), BF16),
         pltpu.VMEM((2 * ROWS, D), BF16),
         pltpu.VMEM((2 * ROWS, D), BF16),
@@ -450,12 +507,14 @@
         pltpu.VMEM((C, NZH, PR, CW), BF16),
         pltpu.VMEM((C, NY, PR, CW), BF16),
         pltpu.VMEM((C, PR, CW), BF16),
+        pltpu.VMEM((2, C, R1 // 2, CW), F32),
         pltpu.VMEM((ROWS, D), F32),
         pltpu.VMEM((ROWS, D), F32),
         pltpu.VMEM((2, ROWS, D), BF16),
         pltpu.VMEM((2, ROWS, D), BF16),
         pltpu.VMEM((2, NX, 8, 128), F32),
         pltpu.VMEM((4, 8, 128), F32),
+        pltpu.VMEM((8, D), F32),
         pltpu.VMEM((4, 8, 128), F32),
         pltpu.VMEM((4, 8, 128), F32),
         pltpu.VMEM((4, 8, 128), F32),
@@ -478,9 +537,9 @@
         out_shape=(
             jax.ShapeDtypeStruct((ROWS, D), BF16),
             jax.ShapeDtypeStruct((ROWS, D), BF16),
-            jax.ShapeDtypeStruct((2, C, 48, CW), BF16),
-            jax.ShapeDtypeStruct((192, D), BF16),
-            jax.ShapeDtypeStruct((8, 128), F32),
+            jax.ShapeDtypeStruct((48, H), F32),
+            jax.ShapeDtypeStruct((192, D), F32),
+            jax.ShapeDtypeStruct((1, 48), F32),
         ),
         in_specs=[vmem, vmem, vmem, smem, vmem, vmem, vmem],
         out_specs=(vmem,) * 5,
@@ -489,16 +548,13 @@
             collective_id=0, has_side_effects=True, vmem_limit_bytes=60 << 20
         ),
         cost_estimate=pl.CostEstimate(flops=14 * 10**9, bytes_accessed=10**7, transcendentals=0),
-    )(tok, cot, live_index, live_count, gain, w1, w_second)
-    f = lax.axis_index("fsdp")
-    grad_first = g1.reshape(2, C, 48, 8, HS).transpose(2, 3, 0, 1, 4).reshape(48, H).astype(F32)
-    grad_gain = lax.dynamic_slice(gg, (f // 2, 48 * (f % 2)), (1, 48)).reshape(48)
+    )(tok, cot, live_index, live_count, norm_gain.reshape(1, 48), w_first, w_second)
     return (
         out.reshape(images, patches, width),
         grad.reshape(images, patches, width),
-        grad_first,
-        g2.astype(F32),
-        grad_gain,
+        g1,
+        g2,
+        gg.reshape(48),
     )
 
 

time: 143 us -> 121 us (0.85)
  Pallas kernels: 127 us -> 112 us
  local copies, waits for them, and re-layouts: 13.6 us -> 6.09 us
    pallas_call x1, Pallas kernels: 127 us -> 112 us  [body(): pl.pallas_call(kernel, out_shape=(jax.ShapeDtypeStruct((ROWS, D), BF16),...]
    convert_element_type x2 -> x0, local copies, waits for them, and re-layouts: 3.46 us -> none  [body(): g1.reshape(2, C, 48, 8, HS).transpose(2, 3, 0, 1, 4).reshape(48, H)]
    reshape x2 -> x0, local copies, waits for them, and re-layouts: 2.81 us -> none  [the longest x1 1.54 us: body(): w_first.reshape(48, 8, 2, C, HS).transpose(2, 3, 0, 1, 4)]
    unnamed x12 -> x13, local copies, waits for them, and re-layouts: 5.87 us -> 6.09 us
where the time goes in v2:
time: 121 us; the launch traced here: 119 us
  Pallas kernels  112 us (93%)
  local copies, waits for them, and re-layouts  6.09 us (5%)
    pallas_call x1, Pallas kernels, body(): pl.pallas_call(kernel, out_shape=(jax.ShapeDtypeStruct((ROWS, D), BF16),...  112 us
    unnamed x13, local copies, waits for them, and re-layouts  6.09 us

profile of v2, /device:TPU:1, one launch (start us, length us, event | category | flops | bytes accessed | tf_op | source)
XLA Modules:
  0.0 118.8 jit_solution(14906771945303836281)
XLA Ops:
  0.6 112.0 %shard_map.110 = (bf16[512,768]{1,0:T(8,128)(2,1)}, bf16[512,768]{1,0:T(8,128)(2,1)}, f32[48,3072]{1,0:T(8,128)}, f32[192,768]{1,0:T(8,128)}, f32[1,48]{1,0:T(1,128)}) custom-call(bf16[512,768]{1,0:T(8,128)(2,1)} %bitcast.8, bf16[512,768]{1,0:T(8,128)(2,1)} %bitcast.9, s32[2,256]{1,0:T(2,128)} %idx.1, s32[2]{0:T(128)} %cnt.1, bf16[1,48]{1,0:T(2,128)(2,1)} %bitcast.10, ...), custom_call_target="tpu_custom_call" | custom-call | flops 14000000000 | bytes 10000000 | tf_op jit(solution)/shard_map/pallas_call | solution.py:535
  112.7 0.0 copy-start
  112.7 2.1 %copy.17 = bf16[2,256,768]{2,1,0:T(8,128)(2,1)} copy(bf16[2,256,768]{2,1,0:T(8,128)(2,1)} %bitcast.7) | data formatting | bytes 1572864
  114.8 0.0 copy-done
  114.8 0.0 copy-start.2
  114.8 0.9 copy.18
  115.7 0.5 copy-done.2
  116.2 0.0 copy-start.1
  116.2 0.8 copy.19
  117.0 0.5 copy-done.1
  117.4 0.0 copy-start.3
  117.4 0.8 copy.20
  118.3 0.0 copy-done.3
  118.3 0.5 copy.21
Async XLA Ops:
  112.7 2.1 %copy-start = (bf16[512,768]{1,0:T(8,128)(2,1)S(1)}, bf16[512,768]{1,0:T(8,128)(2,1)}, u32[]{:S(2)}) copy-start(bf16[512,768]{1,0:T(8,128)(2,1)} %get-tuple-element.11) | copy-start | bytes 2359300
  114.8 1.3 %copy-start.2 = (f32[48,3072]{1,0:T(8,128)S(1)}, f32[48,3072]{1,0:T(8,128)}, u32[]{:S(2)}) copy-start(f32[48,3072]{1,0:T(8,128)} %get-tuple-element.22) | copy-start | bytes 1769476
  116.2 1.3 %copy-start.1 = (f32[192,768]{1,0:T(8,128)S(1)}, f32[192,768]{1,0:T(8,128)}, u32[]{:S(2)}) copy-start(f32[192,768]{1,0:T(8,128)} %get-tuple-element.23) | copy-start | bytes 1769476
  117.4 0.8 copy-start.3

commit v3 on v2

--- a/solution.py
+++ b/solution.py
@@ -14,7 +14,7 @@
 MESH = pl.DeviceIdType.MESH
 NX, NY, NZH = 4, 4, 4
 D, H, ROWS, PATCHES = 768, 3072, 512, 256
-AHEAD = 2
+SPLIT = 4
 C = 6
 HS = 192 // C
 CW = 8 * HS
@@ -33,8 +33,8 @@
 def kernel(tok, cot, idx, cnt, gain, w_in, w2, o_out, o_grad, o_g1, o_g2, o_gain,
            w1, wg, tk, ct, nrm, nt, nf, inv_s, flag_s, hid, bb, buf, r1, s1, r2, s2, r3, r4, fin, gx,
            go, po, pb, px, rx, gt, gsum, gacc, gz, gxx, gyy, gzz,
-           ag_s, ag_r, q1_s, q1_r, q2_s, q2_r, q3_s, q3_r, q4_s, q4_r, q5_s, q5_r, q6_s, q6_r,
-           w_s, w_r, l_s, t_s, t_r, gg_s, gg_r, p_s, p_r, a_s, a_r):
+           ag_s, ag_r, az_s, az_r, ay_s, ay_r, q1_s, q1_r, q2_s, q2_r, q3_s, q3_r, q4_s, q4_r, q5_s, q5_r, q6_s, q6_r,
+           w_s, w_r, t_s, t_r, gg_s, gg_r, p_s, p_r, a_s, a_r):
     dp, f = lax.axis_index("dp"), lax.axis_index("fsdp")
     x, zl, k = lax.div(f, jnp.int32(4)), rem(lax.div(f, jnp.int32(2)), 2), rem(f, 2)
     zh, y = lax.div(dp, jnp.int32(4)), rem(dp, 4)
@@ -78,43 +78,63 @@
     def hidden_block(core, c, qs):
         return (2 * qs + core) * C + c
 
+    gains_own = jnp.broadcast_to(gain[...].astype(F32), (8, 48))
+    gsum[0] = jnp.zeros((8, 128), F32)
     for core in range(2):
+
+        @pl.when(k == core)
+        def _():
+            gsum[0, :, 48 * core : 48 * (core + 1)] = gains_own
+
+    gacc[...] = jnp.zeros((8, D), F32)
+    y_odd = rem(y, 2) == 1
+
+    @pl.when(jnp.logical_not(y_odd))
+    def _():
+        for core in range(2):
+            for c in range(C):
+                for part in range(CW // 128):
+                    pieces = []
+                    for i in range(per):
+                        block = hidden_block(core, c, per * part + i)
+                        start = block // per * 128
+                        pieces.append((w_in[:, start : start + 128].astype(F32), block % per))
+                    w1[core, c, :, 128 * part : 128 * (part + 1)] = gather_lanes(pieces).astype(BF16)
+
+    @pl.when(y_odd)
+    def _():
         for c in range(C):
-            for part in range(CW // 128):
-                pieces = []
-                for i in range(per):
-                    block = hidden_block(core, c, per * part + i)
-                    start = block // per * 128
-                    pieces.append((w_in[:, start : start + 128].astype(F32), block % per))
-                w1[core, c, :, 128 * part : 128 * (part + 1)] = gather_lanes(pieces).astype(BF16)
-    gsum[0] = jnp.zeros((8, 128), F32)
-    gsum[0, :, 0:48] = jnp.broadcast_to(gain[...].astype(F32), (8, 48))
-    gacc[...] = jnp.zeros((8, D), F32)
+            for n in range(NB):
+                wg[c, zl, x, R1 + HS * n : R1 + HS * (n + 1), :] = w2[
+                    HS * c : HS * (c + 1), CW * n : CW * (n + 1)
+                ]
+
     pl.semaphore_wait(barrier, len(everyone))
 
+    send(gsum.at[0], gsum.at[1], gg_s.at[0], gg_r.at[0], partner)
     mine = pl.ds(pl.multiple_of(R1 // 2 * k, 16), R1 // 2)
     other = pl.ds(pl.multiple_of(R1 // 2 * (1 - k), 16), R1 // 2)
-    send(w1.at[1 - k], wg.at[:, q, mine, :], w_s, w_r, partner)
-    own = pltpu.make_async_copy(w1.at[k], wg.at[:, q, mine, :], l_s)
-    own.start()
-    g_own = gsum[0]
-    g_own = jnp.where(k == 1, pltpu.roll(g_own, 48, 1), g_own)
-    gsum[0] = g_own
-    send(gsum.at[0], gsum.at[1], gg_s.at[0], gg_r.at[0], partner)
-    for c in range(C):
-        for n in range(NB):
-            wg[c, q, R1 + HS * n : R1 + HS * (n + 1), :] = w2[HS * c : HS * (c + 1), CW * n : CW * (n + 1)]
-    own.wait()
-    got(wg.at[:, q, other, :], w_r)
-
-    def first_sends(c, carry):
+
+    @pl.when(jnp.logical_not(y_odd))
+    def _():
+        send(w1.at[1 - k], wg.at[:, zl, x, mine, :], w_s, w_r, partner)
+        for c in range(C):
+            wg[c, zl, x, mine, :] = w1[k, c]
+        got(wg.at[:, zl, x, other, :], w_r)
+
+    half = rem(y, 2)
+    my_half = pl.ds(pl.multiple_of(SR // 2 * half, 16), SR // 2)
+    its_half = pl.ds(pl.multiple_of(SR // 2 * (1 - half), 16), SR // 2)
+
+    def pick(cond, a, b):
+        return tuple(jnp.where(cond, i, j) for i, j in zip(a, b))
+
+    def first_sends(c):
+        block = wg.at[c, zl, x, my_half]
         for i in range(1, NX):
-            send(wg.at[c, q], wg.at[c, q], ag_s.at[c, i - 1], ag_r.at[c, i - 1], xp[i - 1])
-        to = tuple(jnp.where(x < 2, a, b) for a, b in zip(near, far))
-        send(wg.at[c, q], wg.at[c, q], ag_s.at[c, 3], ag_r.at[c, 3 + x], to)
-        return carry
-
-    lax.fori_loop(0, AHEAD, first_sends, 0)
+            send(block, block, ag_s.at[c, i - 1], ag_r.at[c, i - 1], xp[i - 1])
+
+    first_sends(0)
 
     got(gsum.at[1], gg_r.at[0])
     gt[zl, x] = gsum[0] + gsum[1]
@@ -138,18 +158,29 @@
     send(tk.at[here], tk.at[here], t_s.at[0], t_r.at[0], partner)
     send(ct.at[here], ct.at[here], t_s.at[1], t_r.at[1], partner)
 
-    def forward(c):
+    def swap(c, kind, at):
+        for i, to in enumerate((yp[0], yp[2])):
+            block = wg.at[c, kind, 2 * i : 2 * i + 2, my_half]
+            send(block, block, ay_s.at[c, 2 * at + i], ay_r.at[c, 2 * at + i], to)
+
+    def forward_x(c):
         for i in range(1, NX):
-            xs = rem(x + NX - i, NX)
-            qs = xs * 2 + zl
-            got(wg.at[c, qs], ag_r.at[c, i - 1])
-            to = tuple(jnp.where(xs < 2, a, b) for a, b in zip(near, far))
-            send(wg.at[c, qs], wg.at[c, qs], ag_s.at[c, 3 + i], ag_r.at[c, 3 + xs], to)
+            got(wg.at[c, zl, rem(x + NX - i, NX), my_half], ag_r.at[c, i - 1])
+        for i, to in enumerate((near, far)):
+            block = wg.at[c, zl, 2 * i : 2 * i + 2, my_half]
+            send(block, block, az_s.at[c, i], az_r.at[c, i], to)
+        swap(c, zl, 0)
+
+    def forward_z(c):
+        for i in range(2):
+            got(wg.at[c, 1 - zl, 2 * i : 2 * i + 2, my_half], az_r.at[c, i])
+        swap(c, 1 - zl, 1)
 
     for i in range(1, NX):
         got(gt.at[zl, rem(x + NX - i, NX)], gg_r.at[i])
     send(gt.at[zl], gt.at[zl], gg_s.at[4], gg_r.at[4], near)
-    forward(0)
+    forward_x(0)
+    first_sends(1)
     got(gt.at[1 - zl], gg_r.at[4])
     got(tk.at[there], t_r.at[0])
     got(ct.at[there], t_r.at[1])
@@ -179,17 +210,21 @@
         return carry
 
     lax.fori_loop(0, 4, norm_step, 0)
+    forward_z(0)
+    forward_x(1)
+    first_sends(2)
 
     def first_of(c):
-        return wg[c, :, 0:R1, :].reshape(D, CW)
+        return jnp.concatenate([wg[c, qs % 2, qs // 2, 0:R1, :] for qs in range(8)], axis=0)
 
     def second_of(c, n):
-        return wg[c, :, R1 + HS * n : R1 + HS * (n + 1), :].reshape(CW, CW)
+        rows = slice(R1 + HS * n, R1 + HS * (n + 1))
+        return jnp.concatenate([wg[c, qs % 2, qs // 2, rows, :] for qs in range(8)], axis=0)
 
     def grads(c):
         for i in range(4):
-            qs = 2 * i + 1 - zl
-            got(wg.at[c, qs], ag_r.at[c, 3 + i])
+            kind, at = zl if i < 2 else 1 - zl, i % 2
+            got(wg.at[c, kind, 2 * at : 2 * at + 2, its_half], ay_r.at[c, i])
 
         def step(m, carry):
             rows = pl.ds(pl.multiple_of(256 * m, 256), 256)
@@ -213,7 +248,9 @@
         lax.fori_loop(0, 4, step, 0)
         for part in range(2):
             term = jnp.dot(nt[384 * part : 384 * (part + 1), :], bb[c], preferred_element_type=F32)
-            own_rows = wg[c, 4 * part : 4 * (part + 1), 0:R1, :].reshape(384, CW)
+            own_rows = jnp.concatenate(
+                [wg[c, qs % 2, qs // 2, 0:R1, :] for qs in range(4 * part, 4 * part + 4)], axis=0
+            )
             product = term * own_rows.astype(F32)
             high = product.astype(BF16)
             low = (product - high.astype(F32)).astype(BF16)
@@ -257,25 +294,43 @@
             part = pl.ds(pl.multiple_of(PR * rem(y + i, NY), 16), PR)
             send(s2.at[c, part], r3.at[c, i - 1], q3_s.at[c, i - 1], q3_r.at[c, i - 1], yp[i - 1])
 
-    def along_y(c):
+    def along_y(c, last=False):
         for i in range(NY - 1):
             got(r3.at[c, i], q3_r.at[c, i])
         total = s2[c, pl.ds(pl.multiple_of(PR * y, 16), PR), :].astype(F32)
         for i in range(NY - 1):
             total = total + r3[c, i].astype(F32)
-        r4[c, zh] = total.astype(BF16)
-        for i in range(1, NZH):
-            send(r4.at[c, zh], r4.at[c, zh], q4_s.at[c, i - 1], q4_r.at[c, i - 1], zp[i - 1])
+        if last:
+            r4[c, zh] = total.astype(BF16)
+            for i in range(1, NZH):
+                send(r4.at[c, zh], r4.at[c, zh], q4_s.at[c, i - 1], q4_r.at[c, i - 1], zp[i - 1])
+        else:
+            r4[c, 0] = total.astype(BF16)
+            to = pick(jnp.logical_xor(rem(zh, 2) == 0, rem(c, 2) == 0), zp[2], zp[0])
+            send(r4.at[c, 0], r4.at[c, 1], q4_s.at[c, 0], q4_r.at[c, 0], to)
+
+    def spread_y(c, total):
+        fin[c, y] = total.astype(BF16)
+        for i in range(1, NY):
+            send(fin.at[c, y], fin.at[c, y], q5_s.at[c, i - 1], q5_r.at[c, i - 1], yp[i - 1])
+
+    def along_z_hi_first(c):
+        got(r4.at[c, 1], q4_r.at[c, 0])
+        r4[c, 2] = (r4[c, 0].astype(F32) + r4[c, 1].astype(F32)).astype(BF16)
+        to = pick(jnp.logical_xor(rem(zh, 2) == 0, rem(c, 2) == 0), zp[0], zp[2])
+        send(r4.at[c, 2], r4.at[c, 3], q4_s.at[c, 1], q4_r.at[c, 1], to)
 
     def along_z_hi(c):
+        got(r4.at[c, 3], q4_r.at[c, 1])
+        spread_y(c, r4[c, 2].astype(F32) + r4[c, 3].astype(F32))
+
+    def along_z_hi_last(c):
         for i in range(1, NZH):
             got(r4.at[c, rem(zh + NZH - i, NZH)], q4_r.at[c, i - 1])
         total = r4[c, 0].astype(F32)
         for i in range(1, NZH):
             total = total + r4[c, i].astype(F32)
-        fin[c, y] = total.astype(BF16)
-        for i in range(1, NY):
-            send(fin.at[c, y], fin.at[c, y], q5_s.at[c, i - 1], q5_r.at[c, i - 1], yp[i - 1])
+        spread_y(c, total)
 
     def back_y(c):
         for i in range(1, NY):
@@ -287,45 +342,45 @@
         for n in range(NB):
             o_g2[rows, CW * n : CW * (n + 1)] = second[HS * n : HS * (n + 1), :].astype(F32)
 
-    def out_rows(start):
+    def out_rows(start, first, end):
         rows = pl.ds(pl.multiple_of(start, 256), 256)
         parts = []
         for n in range(NB):
             total = jnp.zeros((256, CW), F32)
-            for c in range(C):
+            for c in range(first, end):
                 total = total + jnp.dot(hid[c, rows, :], second_of(c, n), preferred_element_type=F32)
             parts.append(total)
-        return parts
-
-    def back_rows(start):
+        return jnp.concatenate(parts, axis=1)
+
+    def back_rows(start, first, end):
         rows = pl.ds(pl.multiple_of(start, 256), 256)
         total = jnp.zeros((256, D), F32)
-        for c in range(C):
+        for c in range(first, end):
             total = total + lax.dot_general(
                 bb[c, rows, :], first_of(c), (((1,), (1,)), ((), ())), preferred_element_type=F32
             )
         return total
 
-    def tail_out():
+    def tail_out(first, end):
         def step(m, carry):
+            m = lax.rem(m + 2 * (1 - k), 4)
             rows = pl.ds(pl.multiple_of(256 * m, 256), 256)
-            for n, part in enumerate(out_rows(ROWS * (1 - k) + 256 * m)):
-                px[0, rows, CW * n : CW * (n + 1)] = part.astype(BF16)
-            px[1, rows, :] = back_rows(ROWS * (1 - k) + 256 * m).astype(BF16)
+            mixed, back = out_rows(256 * m, first, end), back_rows(256 * m, first, end)
+            if first > 0:
+                mixed, back = mixed + po[rows, :], back + pb[rows, :]
+            po[rows, :] = mixed
+            pb[rows, :] = back
             return carry
 
+        if first == 0:
+            lax.fori_loop(0, 4, step, 0)
+            return
         lax.fori_loop(0, 2, step, 0)
+        px[0] = po[there, :].astype(BF16)
+        px[1] = pb[there, :].astype(BF16)
         for i in range(2):
             send(px.at[i], rx.at[i], p_s.at[i], p_r.at[i], partner)
-
-        def step(m, carry):
-            rows = pl.ds(pl.multiple_of(256 * m, 256), 256)
-            for n, part in enumerate(out_rows(ROWS * k + 256 * m)):
-                po[rows, CW * n : CW * (n + 1)] = part
-            pb[rows, :] = back_rows(ROWS * k + 256 * m)
-            return carry
-
-        lax.fori_loop(0, 2, step, 0)
+        lax.fori_loop(2, 4, step, 0)
 
     def tail_rows():
         for i in range(2):
@@ -336,11 +391,11 @@
             at = pl.ds(pl.multiple_of(ROWS * k + 128 * m, 128), 128)
             live = flag_s[rows, :][:, 0:1] > 0
             plain = tok[rows, :].astype(F32)
-            mixed = plain + (po[rows, :] + rx[0, rows, :].astype(F32))
+            mixed = plain + (po[at, :] + rx[0, rows, :].astype(F32))
             o_out[rows, :] = jnp.where(live, mixed, plain).astype(BF16)
             normed = nf[at, :]
             inverse = inv_s[at, :][:, 0:1]
-            back = pb[rows, :] + rx[1, rows, :].astype(F32)
+            back = pb[at, :] + rx[1, rows, :].astype(F32)
             scaled = back * gains
             first = jnp.mean(scaled, axis=1, keepdims=True)
             second = jnp.mean(scaled * normed, axis=1, keepdims=True)
@@ -396,29 +451,96 @@
         row = jnp.where(k == 1, pltpu.roll(row, 80, 1), row)
         o_gain[...] = row[0:1, 0:48]
 
+    def gather_core(c):
+        if c in taken:
+            return
+        taken.add(c)
+        got(gx.at[c], q6_r.at[c])
+        go[1 - k, c] = gx[c].astype(F32)
+
+    taken = set()
+
+    def drain(late):
+        def each(first, end, work):
+            def step(c, carry):
+                work(c)
+                return carry
+
+            lax.fori_loop(first, end, step, 0)
+
+        def weights(c):
+            for i in range(NX - 1):
+                got(wg.at[c, zl, x, my_half], ag_s.at[c, i])
+            for i in range(2):
+                got(wg.at[c, zl, 0:2, my_half], az_s.at[c, i])
+                got(r1.at[c, 0:2], q1_s.at[c, i])
+            for i in range(4):
+                got(wg.at[c, zl, 0:2, my_half], ay_s.at[c, i])
+
+        def by_x(c):
+            for i in range(3):
+                got(r2.at[c, i], q2_s.at[c, i])
+
+        def by_y(c):
+            for i in range(3):
+                got(r3.at[c, i], q3_s.at[c, i])
+
+        def by_z_hi(c):
+            for i in range(2):
+                got(r4.at[c, 0], q4_s.at[c, i])
+
+        def by_back(c):
+            for i in range(3):
+                got(fin.at[c, y], q5_s.at[c, i])
+            got(gx.at[c], q6_s.at[c])
+
+        if not late:
+            each(0, C, weights)
+            each(0, C - 1, by_x)
+            each(0, C - 2, by_y)
+            each(0, C - 4, by_z_hi)
+
+            @pl.when(jnp.logical_not(y_odd))
+            def _():
+                got(wg.at[:, zl, x, mine, :], w_s)
+
+            for i in range(2):
+                got(tk.at[here], t_s.at[i])
+                got(px.at[i], p_s.at[i])
+            for i in range(4):
+                got(gsum.at[0], gg_s.at[i])
+            got(gt.at[zl], gg_s.at[4])
+            return
+        by_x(C - 1)
+        each(C - 2, C, by_y)
+        each(C - 4, C, by_z_hi)
+        got(r4.at[C - 1, 0], q4_s.at[C - 1, 2])
+        each(0, C, by_back)
+        for i in range(11):
+            got(gz.at[0], a_s.at[i])
+
     def slot(t, carry):
-        @pl.when(t + AHEAD < C)
+        @pl.when(t + 2 < C)
         def _():
-            first_sends(t + AHEAD, 0)
+            forward_x(t + 2)
+
+        @pl.when(t + 3 < C)
+        def _():
+            first_sends(t + 3)
 
         @pl.when(t + 1 < C)
         def _():
-            forward(t + 1)
+            forward_z(t + 1)
 
         @pl.when(t < C)
         def _():
             grads(t)
 
-        @pl.when(t == C)
+        @pl.when(t == SPLIT)
         def _():
-            gain_core()
-            tail_out()
-
-        @pl.when(t == C + 1)
-        def _():
-            tail_rows()
-
-        for late, work in ((1, along_z_lo), (2, along_x), (3, along_y), (4, along_z_hi), (5, back_y)):
+            tail_out(0, SPLIT)
+
+        for late, work in ((1, along_z_lo), (2, along_x), (3, along_y), (4, along_z_hi_first), (5, along_z_hi), (6, back_y)):
 
             @pl.when(jnp.logical_and(t >= late, t < C + late))
             def _():
@@ -426,37 +548,44 @@
 
         return carry
 
-    lax.fori_loop(0, C + 2, slot, 0)
+    lax.fori_loop(0, C, slot, 0)
+    gain_core()
+    tail_out(SPLIT, C)
+    along_x(C - 2)
+    along_z_lo(C - 1)
     gain_z_lo()
-    along_y(C - 1)
+    along_y(C - 3)
+    along_z_hi_first(C - 4)
+    along_z_hi(C - 5)
+    back_y(C - 6)
+    tail_rows()
+    drain(late=False)
+    along_x(C - 1)
+    gain_x()
+    along_y(C - 2)
+    along_z_hi_first(C - 3)
+    along_z_hi(C - 4)
+    back_y(C - 5)
+    gather_core(0)
+    along_y(C - 1, last=True)
+    gain_y()
+    along_z_hi_first(C - 2)
+    along_z_hi(C - 3)
+    back_y(C - 4)
+    gather_core(1)
+    along_z_hi_last(C - 1)
+    gain_z_hi()
     along_z_hi(C - 2)
     back_y(C - 3)
-    gain_x()
-    along_z_hi(C - 1)
-    gain_y()
+    gather_core(2)
     back_y(C - 2)
-    gain_z_hi()
+    gain_last()
+    gather_core(3)
     back_y(C - 1)
-    gain_last()
-
-    def last(c, carry):
-        got(gx.at[c], q6_r.at[c])
-        go[1 - k, c] = gx[c].astype(F32)
-        for i in range(4):
-            got(wg.at[c, q], ag_s.at[c, i])
-        for i in range(1, NX):
-            got(wg.at[c, q], ag_s.at[c, 3 + i])
-        got(r1.at[c, 0:2], q1_s.at[c, 0])
-        got(r1.at[c, 2:4], q1_s.at[c, 1])
-        for i in range(3):
-            got(r2.at[c, i], q2_s.at[c, i])
-            got(r3.at[c, i], q3_s.at[c, i])
-            got(r4.at[c, zh], q4_s.at[c, i])
-            got(fin.at[c, y], q5_s.at[c, i])
-        got(gx.at[c], q6_s.at[c])
-        return carry
-
-    lax.fori_loop(0, C, last, 0)
+
+    drain(late=True)
+    for c in range(C):
+        gather_core(c)
     place = {}
     for core in range(2):
         for c in range(C):
@@ -469,15 +598,12 @@
             start = qs // per * 128
             pieces.append((go[core, c, :, start : start + 128], qs % per))
         o_g1[:, 128 * block : 128 * (block + 1)] = gather_lanes(pieces)
-    got(wg.at[:, q, mine, :], w_s)
-    for i in range(2):
-        got(tk.at[here], t_s.at[i])
-        got(px.at[i], p_s.at[i])
-    for i in range(4):
-        got(gsum.at[0], gg_s.at[i])
-    got(gt.at[zl], gg_s.at[4])
-    for i in range(11):
-        got(gz.at[0], a_s.at[i])
+
+
+def place_kernel(*refs):
+    count = len(refs) // 2
+    for i in range(count):
+        refs[count + i][...] = refs[i][...]
 
 
 def body(tokens, cotangent, live_index, live_count, norm_gain, w_first, w_second):
@@ -488,7 +614,7 @@
     dma = pltpu.SemaphoreType.DMA
     scratch = [
         pltpu.VMEM((2, C, R1 // 2, CW), BF16),
-        pltpu.VMEM((C, 8, SR, CW), BF16),
+        pltpu.VMEM((C, 2, NX, SR, CW), BF16),
         pltpu.VMEM((2 * ROWS, D), BF16),
         pltpu.VMEM((2 * ROWS, D), BF16),
         pltpu.VMEM((2 * ROWS, D), BF16),
@@ -508,8 +634,8 @@
         pltpu.VMEM((C, NY, PR, CW), BF16),
         pltpu.VMEM((C, PR, CW), BF16),
         pltpu.VMEM((2, C, R1 // 2, CW), F32),
-        pltpu.VMEM((ROWS, D), F32),
-        pltpu.VMEM((ROWS, D), F32),
+        pltpu.VMEM((2 * ROWS, D), F32),
+        pltpu.VMEM((2 * ROWS, D), F32),
         pltpu.VMEM((2, ROWS, D), BF16),
         pltpu.VMEM((2, ROWS, D), BF16),
         pltpu.VMEM((2, NX, 8, 128), F32),
@@ -519,14 +645,16 @@
         pltpu.VMEM((4, 8, 128), F32),
         pltpu.VMEM((4, 8, 128), F32),
         pltpu.VMEM((4, 8, 128), F32),
-        dma((C, 7)), dma((C, 7)),
+        dma((C, 3)), dma((C, 3)),
+        dma((C, 2)), dma((C, 2)),
+        dma((C, 4)), dma((C, 4)),
         dma((C, 2)), dma((C, 2)),
         dma((C, 3)), dma((C, 3)),
         dma((C, 3)), dma((C, 3)),
         dma((C, 3)), dma((C, 3)),
         dma((C, 3)), dma((C, 3)),
         dma((C,)), dma((C,)),
-        dma, dma, dma,
+        dma, dma,
         dma((2,)), dma((2,)),
         dma((5,)), dma((5,)),
         dma((2,)), dma((2,)),
@@ -549,6 +677,13 @@
         ),
         cost_estimate=pl.CostEstimate(flops=14 * 10**9, bytes_accessed=10**7, transcendentals=0),
     )(tok, cot, live_index, live_count, norm_gain.reshape(1, 48), w_first, w_second)
+    made = (out, grad, g1, g2, gg)
+    out, grad, g1, g2, gg = pl.pallas_call(
+        place_kernel,
+        out_shape=tuple(jax.ShapeDtypeStruct(v.shape, v.dtype) for v in made),
+        in_specs=[vmem] * 5,
+        out_specs=(vmem,) * 5,
+    )(*made)
     return (
         out.reshape(images, patches, width),
         grad.reshape(images, patches, width),

time: 121 us -> 101 us (0.83); the launches traced: 119 us -> 101 us
  Pallas kernels: 112 us -> 100 us
  local copies, waits for them, and re-layouts: 6.09 us -> 0 us
    pallas_call x1, Pallas kernels: 112 us -> 96.8 us  [body(): pl.pallas_call(kernel, out_shape=(jax.ShapeDtypeStruct((ROWS, D), BF16),...]
    unnamed x13 -> x0, local copies, waits for them, and re-layouts: 6.09 us -> none
    pallas_call x0 -> x1, Pallas kernels: none -> 3.3 us  [body(): pl.pallas_call(place_kernel, out_shape=tuple((jax.ShapeDtypeStruct(v.shap...]
where the time goes in v3:
time: 101 us
  Pallas kernels  100 us (99%)
    pallas_call x1, Pallas kernels, body(): pl.pallas_call(kernel, out_shape=(jax.ShapeDtypeStruct((ROWS, D), BF16),...  96.8 us
    pallas_call x1, Pallas kernels, body(): pl.pallas_call(place_kernel, out_shape=tuple((jax.ShapeDtypeStruct(v.shap...  3.3 us

profile of v3, /device:TPU:1, one launch (start us, length us, event | category | flops | bytes accessed | tf_op | source)
XLA Modules:
  0.0 100.8 jit_solution(14039095794587734922)
XLA Ops:
  0.6 96.8 %shard_map.110 = (bf16[512,768]{1,0:T(8,128)(2,1)}, bf16[512,768]{1,0:T(8,128)(2,1)}, f32[48,3072]{1,0:T(8,128)}, f32[192,768]{1,0:T(8,128)}, f32[1,48]{1,0:T(1,128)}) custom-call(bf16[512,768]{1,0:T(8,128)(2,1)} %bitcast.6, bf16[512,768]{1,0:T(8,128)(2,1)} %bitcast.7, s32[2,256]{1,0:T(2,128)} %idx.1, s32[2]{0:T(128)} %cnt.1, bf16[1,48]{1,0:T(2,128)(2,1)} %bitcast.10, ...), custom_call_target="tpu_custom_call" | custom-call | flops 14000000000 | bytes 10000000 | tf_op jit(solution)/shard_map/pallas_call | solution.py:663
  97.5 3.3 %shard_map.111 = (bf16[512,768]{1,0:T(8,128)(2,1)}, bf16[512,768]{1,0:T(8,128)(2,1)}, f32[48,3072]{1,0:T(8,128)}, f32[192,768]{1,0:T(8,128)}, f32[1,48]{1,0:T(1,128)}) custom-call(bf16[512,768]{1,0:T(8,128)(2,1)} %get-tuple-element.15.refs_0_, bf16[512,768]{1,0:T(8,128)(2,1)} %get-tuple-element.16.refs_1_, f32[48,3072]{1,0:T(8,128)} %get-tuple-element.17.refs_2_, ...), custom_call_target="tpu_custom_call" | custom-call | tf_op jit(solution)/shard_map/pallas_call | solution.py:681

commit v4 on v3

--- a/solution.py
+++ b/solution.py
@@ -15,6 +15,8 @@
 NX, NY, NZH = 4, 4, 4
 D, H, ROWS, PATCHES = 768, 3072, 512, 256
 SPLIT = 4
+GROUPS = ((0, 3), (3, 5), (5, 6))
+LAST = 2
 C = 6
 HS = 192 // C
 CW = 8 * HS
@@ -33,7 +35,7 @@
 def kernel(tok, cot, idx, cnt, gain, w_in, w2, o_out, o_grad, o_g1, o_g2, o_gain,
            w1, wg, tk, ct, nrm, nt, nf, inv_s, flag_s, hid, bb, buf, r1, s1, r2, s2, r3, r4, fin, gx,
            go, po, pb, px, rx, gt, gsum, gacc, gz, gxx, gyy, gzz,
-           ag_s, ag_r, az_s, az_r, ay_s, ay_r, q1_s, q1_r, q2_s, q2_r, q3_s, q3_r, q4_s, q4_r, q5_s, q5_r, q6_s, q6_r,
+           ag_s, ag_r, az_s, az_r, ay_s, ay_r, q1_s, q1_r, q2_s, q2_r, q3_s, q3_r, q4_s, q4l_s, q4_r, q5_s, q5_r, q6_s, q6_r,
            w_s, w_r, t_s, t_r, gg_s, gg_r, p_s, p_r, a_s, a_r):
     dp, f = lax.axis_index("dp"), lax.axis_index("fsdp")
     x, zl, k = lax.div(f, jnp.int32(4)), rem(lax.div(f, jnp.int32(2)), 2), rem(f, 2)
@@ -111,7 +113,7 @@
 
     pl.semaphore_wait(barrier, len(everyone))
 
-    send(gsum.at[0], gsum.at[1], gg_s.at[0], gg_r.at[0], partner)
+    send(gsum.at[0], gsum.at[1], gg_s, gg_r.at[0], partner)
     mine = pl.ds(pl.multiple_of(R1 // 2 * k, 16), R1 // 2)
     other = pl.ds(pl.multiple_of(R1 // 2 * (1 - k), 16), R1 // 2)
 
@@ -132,14 +134,14 @@
     def first_sends(c):
         block = wg.at[c, zl, x, my_half]
         for i in range(1, NX):
-            send(block, block, ag_s.at[c, i - 1], ag_r.at[c, i - 1], xp[i - 1])
+            send(block, block, ag_s, ag_r.at[c], xp[i - 1])
 
     first_sends(0)
 
     got(gsum.at[1], gg_r.at[0])
     gt[zl, x] = gsum[0] + gsum[1]
     for i in range(1, NX):
-        send(gt.at[zl, x], gt.at[zl, x], gg_s.at[i], gg_r.at[i], xp[i - 1])
+        send(gt.at[zl, x], gt.at[zl, x], gg_s, gg_r.at[i], xp[i - 1])
 
     for image in range(2):
         at = lax.broadcasted_iota(jnp.int32, (PATCHES, PATCHES), 0)
@@ -155,35 +157,36 @@
         ct[to, :] = jnp.where(flag > 0, cot[rows, :].astype(F32), 0.0).astype(BF16)
     here = pl.ds(pl.multiple_of(ROWS * k, ROWS), ROWS)
     there = pl.ds(pl.multiple_of(ROWS * (1 - k), ROWS), ROWS)
-    send(tk.at[here], tk.at[here], t_s.at[0], t_r.at[0], partner)
-    send(ct.at[here], ct.at[here], t_s.at[1], t_r.at[1], partner)
-
-    def swap(c, kind, at):
-        for i, to in enumerate((yp[0], yp[2])):
-            block = wg.at[c, kind, 2 * i : 2 * i + 2, my_half]
-            send(block, block, ay_s.at[c, 2 * at + i], ay_r.at[c, 2 * at + i], to)
-
-    def forward_x(c):
-        for i in range(1, NX):
-            got(wg.at[c, zl, rem(x + NX - i, NX), my_half], ag_r.at[c, i - 1])
+    send(tk.at[here], tk.at[here], t_s, t_r, partner)
+    send(ct.at[here], ct.at[here], t_s, t_r, partner)
+
+    def swap(c, kind, spread, to):
+        if spread:
+            for i, ends in enumerate((yp[0], yp[2])):
+                block = wg.at[c, kind, 2 * i : 2 * i + 2, my_half]
+                send(block, block, ay_s, ay_r.at[c], ends)
+        else:
+            block = wg.at[c, kind, :, my_half]
+            send(block, block, ay_s, ay_r.at[c], to)
+
+    def forward_x(c, spread=False):
+        got(wg.at[c, zl, 0 : NX - 1, my_half], ag_r.at[c])
         for i, to in enumerate((near, far)):
             block = wg.at[c, zl, 2 * i : 2 * i + 2, my_half]
-            send(block, block, az_s.at[c, i], az_r.at[c, i], to)
-        swap(c, zl, 0)
-
-    def forward_z(c):
-        for i in range(2):
-            got(wg.at[c, 1 - zl, 2 * i : 2 * i + 2, my_half], az_r.at[c, i])
-        swap(c, 1 - zl, 1)
+            send(block, block, az_s, az_r.at[c], to)
+        swap(c, zl, spread, yp[0])
+
+    def forward_z(c, spread=False):
+        got(wg.at[c, 1 - zl, :, my_half], az_r.at[c])
+        swap(c, 1 - zl, spread, yp[2])
 
     for i in range(1, NX):
         got(gt.at[zl, rem(x + NX - i, NX)], gg_r.at[i])
-    send(gt.at[zl], gt.at[zl], gg_s.at[4], gg_r.at[4], near)
-    forward_x(0)
+    send(gt.at[zl], gt.at[zl], gg_s, gg_r.at[4], near)
+    forward_x(0, spread=True)
     first_sends(1)
     got(gt.at[1 - zl], gg_r.at[4])
-    got(tk.at[there], t_r.at[0])
-    got(ct.at[there], t_r.at[1])
+    got(tk, t_r)
 
     def gain_row():
         total = jnp.zeros((8, D), F32)
@@ -210,7 +213,7 @@
         return carry
 
     lax.fori_loop(0, 4, norm_step, 0)
-    forward_z(0)
+    forward_z(0, spread=True)
     forward_x(1)
     first_sends(2)
 
@@ -222,9 +225,7 @@
         return jnp.concatenate([wg[c, qs % 2, qs // 2, rows, :] for qs in range(8)], axis=0)
 
     def grads(c):
-        for i in range(4):
-            kind, at = zl if i < 2 else 1 - zl, i % 2
-            got(wg.at[c, kind, 2 * at : 2 * at + 2, its_half], ay_r.at[c, i])
+        got(wg.at[c, :, :, its_half], ay_r.at[c])
 
         def step(m, carry):
             rows = pl.ds(pl.multiple_of(256 * m, 256), 256)
@@ -245,7 +246,7 @@
             bb[c, rows, :] = (back * slope).astype(BF16)
             return carry
 
-        lax.fori_loop(0, 4, step, 0)
+        lax.fori_loop(0, 4, step, 0, unroll=True)
         for part in range(2):
             term = jnp.dot(nt[384 * part : 384 * (part + 1), :], bb[c], preferred_element_type=F32)
             own_rows = jnp.concatenate(
@@ -272,75 +273,83 @@
             term = (term * SCALE).astype(BF16)
             for qs in range(8):
                 buf[c, qs % 2, qs // 2, R1 + HS * n : R1 + HS * (n + 1), :] = term[HS * qs : HS * (qs + 1), :]
-        send(buf.at[c, 1 - zl, 0:2], r1.at[c, 0:2], q1_s.at[c, 0], q1_r.at[c, 0], near)
-        send(buf.at[c, 1 - zl, 2:4], r1.at[c, 2:4], q1_s.at[c, 1], q1_r.at[c, 1], far)
+        send(buf.at[c, 1 - zl, 0:2], r1.at[c, 0:2], q1_s, q1_r.at[c], near)
+        send(buf.at[c, 1 - zl, 2:4], r1.at[c, 2:4], q1_s, q1_r.at[c], far)
 
     def along_z_lo(c):
-        got(r1.at[c, 0:2], q1_r.at[c, 0])
-        got(r1.at[c, 2:4], q1_r.at[c, 1])
+        got(r1.at[c], q1_r.at[c])
         for i in range(NX):
             s1[c, i] = (buf[c, zl, i].astype(F32) + r1[c, i].astype(F32)).astype(BF16)
         for i in range(1, NX):
-            send(s1.at[c, rem(x + i, NX)], r2.at[c, i - 1], q2_s.at[c, i - 1], q2_r.at[c, i - 1], xp[i - 1])
+            send(s1.at[c, rem(x + i, NX)], r2.at[c, i - 1], q2_s, q2_r.at[c], xp[i - 1])
 
     def along_x(c):
-        for i in range(NX - 1):
-            got(r2.at[c, i], q2_r.at[c, i])
+        got(r2.at[c], q2_r.at[c])
         total = s1[c, x].astype(F32)
         for i in range(NX - 1):
             total = total + r2[c, i].astype(F32)
         s2[c] = total.astype(BF16)
+
+    def start_y(g):
+        first, end = GROUPS[g]
         for i in range(1, NY):
             part = pl.ds(pl.multiple_of(PR * rem(y + i, NY), 16), PR)
-            send(s2.at[c, part], r3.at[c, i - 1], q3_s.at[c, i - 1], q3_r.at[c, i - 1], yp[i - 1])
-
-    def along_y(c, last=False):
+            send(s2.at[first:end, part], r3.at[i - 1, first:end], q3_s, q3_r.at[g], yp[i - 1])
+
+    def along_y(g):
+        first, end = GROUPS[g]
+        got(r3.at[:, first:end], q3_r.at[g])
+        total = s2[first:end, pl.ds(pl.multiple_of(PR * y, 16), PR), :].astype(F32)
         for i in range(NY - 1):
-            got(r3.at[c, i], q3_r.at[c, i])
-        total = s2[c, pl.ds(pl.multiple_of(PR * y, 16), PR), :].astype(F32)
-        for i in range(NY - 1):
-            total = total + r3[c, i].astype(F32)
-        if last:
-            r4[c, zh] = total.astype(BF16)
+            total = total + r3[i, first:end].astype(F32)
+        if g == LAST:
+            r4[zh, first:end] = total.astype(BF16)
             for i in range(1, NZH):
-                send(r4.at[c, zh], r4.at[c, zh], q4_s.at[c, i - 1], q4_r.at[c, i - 1], zp[i - 1])
+                send(r4.at[zh, first:end], r4.at[zh, first:end], q4l_s, q4_r.at[g, 0], zp[i - 1])
         else:
-            r4[c, 0] = total.astype(BF16)
-            to = pick(jnp.logical_xor(rem(zh, 2) == 0, rem(c, 2) == 0), zp[2], zp[0])
-            send(r4.at[c, 0], r4.at[c, 1], q4_s.at[c, 0], q4_r.at[c, 0], to)
-
-    def spread_y(c, total):
-        fin[c, y] = total.astype(BF16)
+            r4[0, first:end] = total.astype(BF16)
+            to = pick(jnp.logical_xor(rem(zh, 2) == 0, g % 2 == 0), zp[2], zp[0])
+            send(r4.at[0, first:end], r4.at[1, first:end], q4_s, q4_r.at[g, 0], to)
+
+    def spread_y(g, total):
+        first, end = GROUPS[g]
+        fin[y, first:end] = total.astype(BF16)
         for i in range(1, NY):
-            send(fin.at[c, y], fin.at[c, y], q5_s.at[c, i - 1], q5_r.at[c, i - 1], yp[i - 1])
-
-    def along_z_hi_first(c):
-        got(r4.at[c, 1], q4_r.at[c, 0])
-        r4[c, 2] = (r4[c, 0].astype(F32) + r4[c, 1].astype(F32)).astype(BF16)
-        to = pick(jnp.logical_xor(rem(zh, 2) == 0, rem(c, 2) == 0), zp[0], zp[2])
-        send(r4.at[c, 2], r4.at[c, 3], q4_s.at[c, 1], q4_r.at[c, 1], to)
-
-    def along_z_hi(c):
-        got(r4.at[c, 3], q4_r.at[c, 1])
-        spread_y(c, r4[c, 2].astype(F32) + r4[c, 3].astype(F32))
-
-    def along_z_hi_last(c):
-        for i in range(1, NZH):
-            got(r4.at[c, rem(zh + NZH - i, NZH)], q4_r.at[c, i - 1])
-        total = r4[c, 0].astype(F32)
-        for i in range(1, NZH):
-            total = total + r4[c, i].astype(F32)
-        spread_y(c, total)
-
-    def back_y(c):
-        for i in range(1, NY):
-            got(fin.at[c, rem(y + NY - i, NY)], q5_r.at[c, i - 1])
-        send(fin.at[c, 1 - k], gx.at[c], q6_s.at[c], q6_r.at[c], partner)
-        go[k, c] = fin[c, k].astype(F32)
-        second = fin[c, 2:4].reshape(R2, CW)
-        rows = pl.ds(pl.multiple_of(HS * c, HS), HS)
-        for n in range(NB):
-            o_g2[rows, CW * n : CW * (n + 1)] = second[HS * n : HS * (n + 1), :].astype(F32)
+            send(fin.at[y, first:end], fin.at[y, first:end], q5_s, q5_r.at[g], yp[i - 1])
+
+    def along_z_hi_first(g):
+        first, end = GROUPS[g]
+        got(r4.at[1, first:end], q4_r.at[g, 0])
+        r4[2, first:end] = (r4[0, first:end].astype(F32) + r4[1, first:end].astype(F32)).astype(BF16)
+        to = pick(jnp.logical_xor(rem(zh, 2) == 0, g % 2 == 0), zp[0], zp[2])
+        send(r4.at[2, first:end], r4.at[3, first:end], q4_s, q4_r.at[g, 1], to)
+
+    def along_z_hi(g):
+        first, end = GROUPS[g]
+        if g == LAST:
+            got(r4.at[0 : NZH - 1, first:end], q4_r.at[g, 0])
+            total = r4[0, first:end].astype(F32)
+            for i in range(1, NZH):
+                total = total + r4[i, first:end].astype(F32)
+        else:
+            got(r4.at[3, first:end], q4_r.at[g, 1])
+            total = r4[2, first:end].astype(F32) + r4[3, first:end].astype(F32)
+        spread_y(g, total)
+
+    def back_y(g):
+        first, end = GROUPS[g]
+        got(fin.at[0 : NY - 1, first:end], q5_r.at[g])
+        send(fin.at[1 - k, first:end], gx.at[first:end], q6_s, q6_r.at[g], partner)
+        go[k, first:end] = fin[k, first:end].astype(F32)
+        for c in range(first, end):
+            second = fin[2:4, c].reshape(R2, CW).astype(F32)
+            for n in range(NB):
+                o_g2[HS * c : HS * (c + 1), CW * n : CW * (n + 1)] = second[HS * n : HS * (n + 1), :]
+
+    def gather_core(g):
+        first, end = GROUPS[g]
+        got(gx.at[first:end], q6_r.at[g])
+        go[1 - k, first:end] = gx[first:end].astype(F32)
 
     def out_rows(start, first, end):
         rows = pl.ds(pl.multiple_of(start, 256), 256)
@@ -373,18 +382,17 @@
             return carry
 
         if first == 0:
-            lax.fori_loop(0, 4, step, 0)
+            lax.fori_loop(0, 4, step, 0, unroll=True)
             return
-        lax.fori_loop(0, 2, step, 0)
+        lax.fori_loop(0, 2, step, 0, unroll=True)
         px[0] = po[there, :].astype(BF16)
         px[1] = pb[there, :].astype(BF16)
         for i in range(2):
-            send(px.at[i], rx.at[i], p_s.at[i], p_r.at[i], partner)
-        lax.fori_loop(2, 4, step, 0)
+            send(px.at[i], rx.at[i], p_s, p_r, partner)
+        lax.fori_loop(2, 4, step, 0, unroll=True)
 
     def tail_rows():
-        for i in range(2):
-            got(rx.at[i], p_r.at[i])
+        got(rx, p_r)
 
         def step(m, carry):
             rows = pl.ds(pl.multiple_of(128 * m, 128), 128)
@@ -414,32 +422,32 @@
             turned = (pltpu.roll(row, D - 96 * qs, 1) if qs else row)[:, 0:128]
             tile = jnp.where(line == qs, turned, tile)
         gz[0] = tile
-        send(gz.at[0], gz.at[1], a_s.at[0], a_r.at[0], partner)
+        send(gz.at[0], gz.at[1], a_s, a_r.at[0], partner)
 
     def gain_z_lo():
         got(gz.at[1], a_r.at[0])
         gz[2] = gz[0] + gz[1]
-        send(gz.at[2], gz.at[3], a_s.at[1], a_r.at[1], near)
+        send(gz.at[2], gz.at[3], a_s, a_r.at[1], near)
 
     def gain_x():
         got(gz.at[3], a_r.at[1])
         gxx[x] = gz[2] + gz[3]
         for i in range(1, NX):
-            send(gxx.at[x], gxx.at[x], a_s.at[1 + i], a_r.at[1 + i], xp[i - 1])
+            send(gxx.at[x], gxx.at[x], a_s, a_r.at[1 + i], xp[i - 1])
 
     def gain_y():
         for i in range(1, NX):
             got(gxx.at[rem(x + NX - i, NX)], a_r.at[1 + i])
         gyy[y] = gxx[0] + gxx[1] + gxx[2] + gxx[3]
         for i in range(1, NY):
-            send(gyy.at[y], gyy.at[y], a_s.at[4 + i], a_r.at[4 + i], yp[i - 1])
+            send(gyy.at[y], gyy.at[y], a_s, a_r.at[4 + i], yp[i - 1])
 
     def gain_z_hi():
         for i in range(1, NY):
             got(gyy.at[rem(y + NY - i, NY)], a_r.at[4 + i])
         gzz[zh] = gyy[0] + gyy[1] + gyy[2] + gyy[3]
         for i in range(1, NZH):
-            send(gzz.at[zh], gzz.at[zh], a_s.at[7 + i], a_r.at[7 + i], zp[i - 1])
+            send(gzz.at[zh], gzz.at[zh], a_s, a_r.at[7 + i], zp[i - 1])
 
     def gain_last():
         for i in range(1, NZH):
@@ -451,73 +459,27 @@
         row = jnp.where(k == 1, pltpu.roll(row, 80, 1), row)
         o_gain[...] = row[0:1, 0:48]
 
-    def gather_core(c):
-        if c in taken:
-            return
-        taken.add(c)
-        got(gx.at[c], q6_r.at[c])
-        go[1 - k, c] = gx[c].astype(F32)
-
-    taken = set()
-
-    def drain(late):
-        def each(first, end, work):
-            def step(c, carry):
-                work(c)
-                return carry
-
-            lax.fori_loop(first, end, step, 0)
-
-        def weights(c):
-            for i in range(NX - 1):
-                got(wg.at[c, zl, x, my_half], ag_s.at[c, i])
-            for i in range(2):
-                got(wg.at[c, zl, 0:2, my_half], az_s.at[c, i])
-                got(r1.at[c, 0:2], q1_s.at[c, i])
-            for i in range(4):
-                got(wg.at[c, zl, 0:2, my_half], ay_s.at[c, i])
-
-        def by_x(c):
-            for i in range(3):
-                got(r2.at[c, i], q2_s.at[c, i])
-
-        def by_y(c):
-            for i in range(3):
-                got(r3.at[c, i], q3_s.at[c, i])
-
-        def by_z_hi(c):
-            for i in range(2):
-                got(r4.at[c, 0], q4_s.at[c, i])
-
-        def by_back(c):
-            for i in range(3):
-                got(fin.at[c, y], q5_s.at[c, i])
-            got(gx.at[c], q6_s.at[c])
-
-        if not late:
-            each(0, C, weights)
-            each(0, C - 1, by_x)
-            each(0, C - 2, by_y)
-            each(0, C - 4, by_z_hi)
-
-            @pl.when(jnp.logical_not(y_odd))
-            def _():
-                got(wg.at[:, zl, x, mine, :], w_s)
-
-            for i in range(2):
-                got(tk.at[here], t_s.at[i])
-                got(px.at[i], p_s.at[i])
-            for i in range(4):
-                got(gsum.at[0], gg_s.at[i])
-            got(gt.at[zl], gg_s.at[4])
-            return
-        by_x(C - 1)
-        each(C - 2, C, by_y)
-        each(C - 4, C, by_z_hi)
-        got(r4.at[C - 1, 0], q4_s.at[C - 1, 2])
-        each(0, C, by_back)
-        for i in range(11):
-            got(gz.at[0], a_s.at[i])
+    def drain_first():
+        got(r2.at[:, :, 0 : SR // 2], ag_s)
+        got(wg.at[:, 0, :, 0 : SR // 2], az_s)
+        got(wg.at[:, :, :, 0 : SR // 2], ay_s)
+        got(r1, q1_s)
+        got(tk, t_s)
+        got(px, p_s)
+        got(inv_s.at[0:64], gg_s)
+
+        @pl.when(jnp.logical_not(y_odd))
+        def _():
+            got(wg.at[:, zl, x, mine, :], w_s)
+
+    def drain_last():
+        got(r2, q2_s)
+        got(r3, q3_s)
+        got(r4.at[0:2, 0 : GROUPS[LAST][0]], q4_s)
+        got(r4.at[0 : NZH - 1, GROUPS[LAST][0] : C], q4l_s)
+        got(fin.at[0 : NY - 1], q5_s)
+        got(gx, q6_s)
+        got(inv_s.at[0:88], a_s)
 
     def slot(t, carry):
         @pl.when(t + 2 < C)
@@ -540,11 +502,15 @@
         def _():
             tail_out(0, SPLIT)
 
-        for late, work in ((1, along_z_lo), (2, along_x), (3, along_y), (4, along_z_hi_first), (5, along_z_hi), (6, back_y)):
-
-            @pl.when(jnp.logical_and(t >= late, t < C + late))
+        for late, work in ((1, along_z_lo), (2, along_x)):
+
+            @pl.when(t >= late)
             def _():
                 work(t - late)
+
+        @pl.when(t == GROUPS[0][1] + 1)
+        def _():
+            start_y(0)
 
         return carry
 
@@ -552,40 +518,32 @@
     gain_core()
     tail_out(SPLIT, C)
     along_x(C - 2)
+    start_y(1)
+    along_y(0)
     along_z_lo(C - 1)
     gain_z_lo()
-    along_y(C - 3)
-    along_z_hi_first(C - 4)
-    along_z_hi(C - 5)
-    back_y(C - 6)
     tail_rows()
-    drain(late=False)
+    along_z_hi_first(0)
+    along_y(1)
+    drain_first()
     along_x(C - 1)
+    start_y(2)
     gain_x()
-    along_y(C - 2)
-    along_z_hi_first(C - 3)
-    along_z_hi(C - 4)
-    back_y(C - 5)
+    along_z_hi(0)
+    along_z_hi_first(1)
+    along_y(2)
+    gain_y()
+    along_z_hi(1)
+    back_y(0)
+    along_z_hi(2)
+    gain_z_hi()
+    back_y(1)
     gather_core(0)
-    along_y(C - 1, last=True)
-    gain_y()
-    along_z_hi_first(C - 2)
-    along_z_hi(C - 3)
-    back_y(C - 4)
+    gain_last()
     gather_core(1)
-    along_z_hi_last(C - 1)
-    gain_z_hi()
-    along_z_hi(C - 2)
-    back_y(C - 3)
+    back_y(2)
+    drain_last()
     gather_core(2)
-    back_y(C - 2)
-    gain_last()
-    gather_core(3)
-    back_y(C - 1)
-
-    drain(late=True)
-    for c in range(C):
-        gather_core(c)
     place = {}
     for core in range(2):
         for c in range(C):
@@ -629,9 +587,9 @@
         pltpu.VMEM((C, NX, SR, CW), BF16),
         pltpu.VMEM((C, NX - 1, SR, CW), BF16),
         pltpu.VMEM((C, SR, CW), BF16),
-        pltpu.VMEM((C, NY - 1, PR, CW), BF16),
-        pltpu.VMEM((C, NZH, PR, CW), BF16),
-        pltpu.VMEM((C, NY, PR, CW), BF16),
+        pltpu.VMEM((NY - 1, C, PR, CW), BF16),
+        pltpu.VMEM((NZH, C, PR, CW), BF16),
+        pltpu.VMEM((NY, C, PR, CW), BF16),
         pltpu.VMEM((C, PR, CW), BF16),
         pltpu.VMEM((2, C, R1 // 2, CW), F32),
         pltpu.VMEM((2 * ROWS, D), F32),
@@ -645,20 +603,20 @@
         pltpu.VMEM((4, 8, 128), F32),
         pltpu.VMEM((4, 8, 128), F32),
         pltpu.VMEM((4, 8, 128), F32),
-        dma((C, 3)), dma((C, 3)),
-        dma((C, 2)), dma((C, 2)),
-        dma((C, 4)), dma((C, 4)),
-        dma((C, 2)), dma((C, 2)),
-        dma((C, 3)), dma((C, 3)),
-        dma((C, 3)), dma((C, 3)),
-        dma((C, 3)), dma((C, 3)),
-        dma((C, 3)), dma((C, 3)),
-        dma((C,)), dma((C,)),
+        dma, dma((C,)),
+        dma, dma((C,)),
+        dma, dma((C,)),
+        dma, dma((C,)),
+        dma, dma((C,)),
+        dma, dma((3,)),
+        dma, dma, dma((3, 2)),
+        dma, dma((3,)),
+        dma, dma((3,)),
         dma, dma,
-        dma((2,)), dma((2,)),
-        dma((5,)), dma((5,)),
-        dma((2,)), dma((2,)),
-        dma((11,)), dma((11,)),
+        dma, dma,
+        dma, dma((5,)),
+        dma, dma,
+        dma, dma((11,)),
     ]
     out, grad, g1, g2, gg = pl.pallas_call(
         kernel,

time: 101 us -> 98.5 us (0.975)
  Pallas kernels: 100 us -> 97.7 us
    pallas_call x1, Pallas kernels: 96.8 us -> 94.4 us  [body(): pl.pallas_call(kernel, out_shape=(jax.ShapeDtypeStruct((ROWS, D), BF16),...]
where the time goes in v4:
time: 98.5 us; the launch traced here: 98.4 us
  Pallas kernels  97.7 us (99%)
    pallas_call x1, Pallas kernels, body(): pl.pallas_call(kernel, out_shape=(jax.ShapeDtypeStruct((ROWS, D), BF16),...  94.4 us
    pallas_call x1, Pallas kernels, body(): pl.pallas_call(place_kernel, out_shape=tuple((jax.ShapeDtypeStruct(v.shap...  3.3 us

profile of v4, /device:TPU:1, one launch (start us, length us, event | category | flops | bytes accessed | tf_op | source)
XLA Modules:
  0.0 98.4 jit_solution(5223812210723277673)
XLA Ops:
  0.6 94.4 %shard_map.110 = (bf16[512,768]{1,0:T(8,128)(2,1)}, bf16[512,768]{1,0:T(8,128)(2,1)}, f32[48,3072]{1,0:T(8,128)}, f32[192,768]{1,0:T(8,128)}, f32[1,48]{1,0:T(1,128)}) custom-call(bf16[512,768]{1,0:T(8,128)(2,1)} %bitcast.6, bf16[512,768]{1,0:T(8,128)(2,1)} %bitcast.7, s32[2,256]{1,0:T(2,128)} %idx.1, s32[2]{0:T(128)} %cnt.1, bf16[1,48]{1,0:T(2,128)(2,1)} %bitcast.10, ...), custom_call_target="tpu_custom_call" | custom-call | flops 14000000000 | bytes 10000000 | tf_op jit(solution)/shard_map/pallas_call | solution.py:621
  95.1 3.3 %shard_map.111 = (bf16[512,768]{1,0:T(8,128)(2,1)}, bf16[512,768]{1,0:T(8,128)(2,1)}, f32[48,3072]{1,0:T(8,128)}, f32[192,768]{1,0:T(8,128)}, f32[1,48]{1,0:T(1,128)}) custom-call(bf16[512,768]{1,0:T(8,128)(2,1)} %get-tuple-element.15.refs_0_, bf16[512,768]{1,0:T(8,128)(2,1)} %get-tuple-element.16.refs_1_, f32[48,3072]{1,0:T(8,128)} %get-tuple-element.17.refs_2_, ...), custom_call_target="tpu_custom_call" | custom-call | tf_op jit(solution)/shard_map/pallas_call | solution.py:639

commit v5 on v4

--- a/solution.py
+++ b/solution.py
@@ -15,8 +15,7 @@
 NX, NY, NZH = 4, 4, 4
 D, H, ROWS, PATCHES = 768, 3072, 512, 256
 SPLIT = 4
-GROUPS = ((0, 3), (3, 5), (5, 6))
-LAST = 2
+GROUPS = ((0, 2), (2, 4), (4, 5))
 C = 6
 HS = 192 // C
 CW = 8 * HS
@@ -34,8 +33,9 @@
 
 def kernel(tok, cot, idx, cnt, gain, w_in, w2, o_out, o_grad, o_g1, o_g2, o_gain,
            w1, wg, tk, ct, nrm, nt, nf, inv_s, flag_s, hid, bb, buf, r1, s1, r2, s2, r3, r4, fin, gx,
-           go, po, pb, px, rx, gt, gsum, gacc, gz, gxx, gyy, gzz,
-           ag_s, ag_r, az_s, az_r, ay_s, ay_r, q1_s, q1_r, q2_s, q2_r, q3_s, q3_r, q4_s, q4l_s, q4_r, q5_s, q5_r, q6_s, q6_r,
+           e1, eb, sl1, rl2, sl2, rl3, rl4, finl, xg, go, po, pb, px, rx, gt, gsum, gacc, gz, gxx, gyy, gzz,
+           ag_s, ag_r, az_s, az_r, ay_s, ay_r, q1_s, q1_r, q2_s, q2_r, q3_s, q3_r, q4_s, q4_r, q5_s, q5_r, q6_s, q6_r,
+           qe_r, qb_s, qb_r, l2_s, l2_r, l3_s, l3_r, l4_s, l4_r, l5_s, l5_r, l6_s, l6_r,
            w_s, w_r, t_s, t_r, gg_s, gg_r, p_s, p_r, a_s, a_r):
     dp, f = lax.axis_index("dp"), lax.axis_index("fsdp")
     x, zl, k = lax.div(f, jnp.int32(4)), rem(lax.div(f, jnp.int32(2)), 2), rem(f, 2)
@@ -62,7 +62,8 @@
     def got(ref, sem):
         pltpu.make_async_copy(ref, ref, sem).wait()
 
-    everyone = [partner, near, far] + xp + yp + zp
+    near_other, far_other = dev(x, y, z_near, 1 - k), dev(x, y, z_far, 1 - k)
+    everyone = [partner, near, far, near_other, far_other] + xp + yp + zp
     barrier = pltpu.get_barrier_semaphore()
     for peer in everyone:
         pl.semaphore_signal(barrier, inc=1, device_id=peer, device_id_type=MESH)
@@ -169,14 +170,14 @@
             block = wg.at[c, kind, :, my_half]
             send(block, block, ay_s, ay_r.at[c], to)
 
-    def forward_x(c, spread=False):
+    def forward_x(c, spread=True):
         got(wg.at[c, zl, 0 : NX - 1, my_half], ag_r.at[c])
         for i, to in enumerate((near, far)):
             block = wg.at[c, zl, 2 * i : 2 * i + 2, my_half]
             send(block, block, az_s, az_r.at[c], to)
         swap(c, zl, spread, yp[0])
 
-    def forward_z(c, spread=False):
+    def forward_z(c, spread=True):
         got(wg.at[c, 1 - zl, :, my_half], az_r.at[c])
         swap(c, 1 - zl, spread, yp[2])
 
@@ -273,8 +274,18 @@
             term = (term * SCALE).astype(BF16)
             for qs in range(8):
                 buf[c, qs % 2, qs // 2, R1 + HS * n : R1 + HS * (n + 1), :] = term[HS * qs : HS * (qs + 1), :]
-        send(buf.at[c, 1 - zl, 0:2], r1.at[c, 0:2], q1_s, q1_r.at[c], near)
-        send(buf.at[c, 1 - zl, 2:4], r1.at[c, 2:4], q1_s, q1_r.at[c], far)
+        to_odd = jnp.logical_and(c == C - 1, k == 0)
+
+        @pl.when(jnp.logical_not(to_odd))
+        def _():
+            send(buf.at[c, 1 - zl, 0:2], r1.at[c, 0:2], q1_s, q1_r.at[c], near)
+            send(buf.at[c, 1 - zl, 2:4], r1.at[c, 2:4], q1_s, q1_r.at[c], far)
+
+        @pl.when(to_odd)
+        def _():
+            send(buf.at[c, 1 - zl, 0:2], e1.at[0:2], q1_s, qe_r, near_other)
+            send(buf.at[c, 1 - zl, 2:4], e1.at[2:4], q1_s, qe_r, far_other)
+            send(buf.at[c, zl], eb, qb_s, qb_r, partner)
 
     def along_z_lo(c):
         got(r1.at[c], q1_r.at[c])
@@ -302,14 +313,9 @@
         total = s2[first:end, pl.ds(pl.multiple_of(PR * y, 16), PR), :].astype(F32)
         for i in range(NY - 1):
             total = total + r3[i, first:end].astype(F32)
-        if g == LAST:
-            r4[zh, first:end] = total.astype(BF16)
-            for i in range(1, NZH):
-                send(r4.at[zh, first:end], r4.at[zh, first:end], q4l_s, q4_r.at[g, 0], zp[i - 1])
-        else:
-            r4[0, first:end] = total.astype(BF16)
-            to = pick(jnp.logical_xor(rem(zh, 2) == 0, g % 2 == 0), zp[2], zp[0])
-            send(r4.at[0, first:end], r4.at[1, first:end], q4_s, q4_r.at[g, 0], to)
+        r4[0, first:end] = total.astype(BF16)
+        to = pick(jnp.logical_xor(rem(zh, 2) == 0, g % 2 == 0), zp[2], zp[0])
+        send(r4.at[0, first:end], r4.at[1, first:end], q4_s, q4_r.at[g, 0], to)
 
     def spread_y(g, total):
         first, end = GROUPS[g]
@@ -326,15 +332,13 @@
 
     def along_z_hi(g):
         first, end = GROUPS[g]
-        if g == LAST:
-            got(r4.at[0 : NZH - 1, first:end], q4_r.at[g, 0])
-            total = r4[0, first:end].astype(F32)
-            for i in range(1, NZH):
-                total = total + r4[i, first:end].astype(F32)
-        else:
-            got(r4.at[3, first:end], q4_r.at[g, 1])
-            total = r4[2, first:end].astype(F32) + r4[3, first:end].astype(F32)
-        spread_y(g, total)
+        got(r4.at[3, first:end], q4_r.at[g, 1])
+        spread_y(g, r4[2, first:end].astype(F32) + r4[3, first:end].astype(F32))
+
+    def put_second(c, parts):
+        second = parts.reshape(R2, CW).astype(F32)
+        for n in range(NB):
+            o_g2[HS * c : HS * (c + 1), CW * n : CW * (n + 1)] = second[HS * n : HS * (n + 1), :]
 
     def back_y(g):
         first, end = GROUPS[g]
@@ -342,14 +346,83 @@
         send(fin.at[1 - k, first:end], gx.at[first:end], q6_s, q6_r.at[g], partner)
         go[k, first:end] = fin[k, first:end].astype(F32)
         for c in range(first, end):
-            second = fin[2:4, c].reshape(R2, CW).astype(F32)
-            for n in range(NB):
-                o_g2[HS * c : HS * (c + 1), CW * n : CW * (n + 1)] = second[HS * n : HS * (n + 1), :]
+            put_second(c, fin[2:4, c])
 
     def gather_core(g):
         first, end = GROUPS[g]
         got(gx.at[first:end], q6_r.at[g])
         go[1 - k, first:end] = gx[first:end].astype(F32)
+
+    def last_z():
+        @pl.when(k == 1)
+        def _():
+            got(eb, qb_r)
+            got(r1.at[C - 1], q1_r.at[C - 1])
+            got(e1, qe_r)
+            for i in range(NX):
+                sl1[0, i] = (eb[i].astype(F32) + e1[i].astype(F32)).astype(BF16)
+                sl1[1, i] = (buf[C - 1, zl, i].astype(F32) + r1[C - 1, i].astype(F32)).astype(BF16)
+            for i in range(1, NX):
+                send(sl1.at[:, rem(x + i, NX)], rl2.at[i - 1], l2_s, l2_r, xp[i - 1])
+
+    def last_x():
+        @pl.when(k == 1)
+        def _():
+            got(rl2, l2_r)
+            total = sl1[:, x].astype(F32)
+            for i in range(NX - 1):
+                total = total + rl2[i].astype(F32)
+            sl2[...] = total.astype(BF16)
+            for i in range(1, NY):
+                part = pl.ds(pl.multiple_of(PR * rem(y + i, NY), 16), PR)
+                send(sl2.at[:, part], rl3.at[i - 1], l3_s, l3_r, yp[i - 1])
+
+    def last_y():
+        @pl.when(k == 1)
+        def _():
+            got(rl3, l3_r)
+            total = sl2[:, pl.ds(pl.multiple_of(PR * y, 16), PR), :].astype(F32)
+            for i in range(NY - 1):
+                total = total + rl3[i].astype(F32)
+            rl4[zh] = total.astype(BF16)
+            for i in range(1, NZH):
+                send(rl4.at[zh], rl4.at[zh], l4_s, l4_r, zp[i - 1])
+
+    def last_z_hi():
+        @pl.when(k == 1)
+        def _():
+            got(rl4.at[0 : NZH - 1], l4_r)
+            total = rl4[0].astype(F32)
+            for i in range(1, NZH):
+                total = total + rl4[i].astype(F32)
+            finl[y] = total.astype(BF16)
+            for i in range(1, NY):
+                send(finl.at[y], finl.at[y], l5_s, l5_r, yp[i - 1])
+
+    def last_back():
+        @pl.when(k == 1)
+        def _():
+            got(finl.at[0 : NY - 1], l5_r)
+            send(finl.at[0], xg.at[0], l6_s, l6_r, partner)
+            send(finl.at[2:4, 0], xg.at[1], l6_s, l6_r, partner)
+            go[:, C - 1] = finl[1].astype(F32)
+            put_second(C - 1, finl[2:4, 1])
+
+    def last_take():
+        @pl.when(k == 0)
+        def _():
+            got(xg, l6_r)
+            go[:, C - 1] = xg[0].astype(F32)
+            put_second(C - 1, xg[1])
+            got(eb, qb_s)
+
+        @pl.when(k == 1)
+        def _():
+            got(rl2, l2_s)
+            got(rl3, l3_s)
+            got(rl4.at[0 : NZH - 1], l4_s)
+            got(finl.at[0 : NY - 1], l5_s)
+            got(xg, l6_s)
 
     def out_rows(start, first, end):
         rows = pl.ds(pl.multiple_of(start, 256), 256)
@@ -473,12 +546,11 @@
             got(wg.at[:, zl, x, mine, :], w_s)
 
     def drain_last():
-        got(r2, q2_s)
-        got(r3, q3_s)
-        got(r4.at[0:2, 0 : GROUPS[LAST][0]], q4_s)
-        got(r4.at[0 : NZH - 1, GROUPS[LAST][0] : C], q4l_s)
-        got(fin.at[0 : NY - 1], q5_s)
-        got(gx, q6_s)
+        got(r2.at[0 : C - 1], q2_s)
+        got(r3.at[:, 0 : C - 1], q3_s)
+        got(r4.at[0:2, 0 : C - 1], q4_s)
+        got(fin.at[0 : NY - 1, 0 : C - 1], q5_s)
+        got(gx.at[0 : C - 1], q6_s)
         got(inv_s.at[0:88], a_s)
 
     def slot(t, carry):
@@ -508,9 +580,12 @@
             def _():
                 work(t - late)
 
-        @pl.when(t == GROUPS[0][1] + 1)
-        def _():
-            start_y(0)
+        for at, steps in ((3, ((start_y, 0),)), (4, ((along_y, 0),)), (5, ((along_z_hi_first, 0), (start_y, 1)))):
+
+            @pl.when(t == at)
+            def _():
+                for work, g in steps:
+                    work(g)
 
         return carry
 
@@ -518,32 +593,34 @@
     gain_core()
     tail_out(SPLIT, C)
     along_x(C - 2)
-    start_y(1)
-    along_y(0)
-    along_z_lo(C - 1)
+    start_y(2)
+    along_y(1)
+    along_z_hi(0)
+    last_z()
     gain_z_lo()
     tail_rows()
-    along_z_hi_first(0)
-    along_y(1)
-    drain_first()
-    along_x(C - 1)
-    start_y(2)
-    gain_x()
-    along_z_hi(0)
     along_z_hi_first(1)
     along_y(2)
+    drain_first()
+    back_y(0)
+    last_x()
+    gain_x()
+    along_z_hi(1)
+    along_z_hi_first(2)
+    last_y()
     gain_y()
-    along_z_hi(1)
-    back_y(0)
+    gather_core(0)
     along_z_hi(2)
+    back_y(1)
+    last_z_hi()
     gain_z_hi()
-    back_y(1)
-    gather_core(0)
+    back_y(2)
+    gather_core(1)
     gain_last()
-    gather_core(1)
-    back_y(2)
+    gather_core(2)
+    last_back()
     drain_last()
-    gather_core(2)
+    last_take()
     place = {}
     for core in range(2):
         for c in range(C):
@@ -591,6 +668,15 @@
         pltpu.VMEM((NZH, C, PR, CW), BF16),
         pltpu.VMEM((NY, C, PR, CW), BF16),
         pltpu.VMEM((C, PR, CW), BF16),
+        pltpu.VMEM((NX, SR, CW), BF16),
+        pltpu.VMEM((NX, SR, CW), BF16),
+        pltpu.VMEM((2, NX, SR, CW), BF16),
+        pltpu.VMEM((NX - 1, 2, SR, CW), BF16),
+        pltpu.VMEM((2, SR, CW), BF16),
+        pltpu.VMEM((NY - 1, 2, PR, CW), BF16),
+        pltpu.VMEM((NZH, 2, PR, CW), BF16),
+        pltpu.VMEM((NY, 2, PR, CW), BF16),
+        pltpu.VMEM((2, 2, PR, CW), BF16),
         pltpu.VMEM((2, C, R1 // 2, CW), F32),
         pltpu.VMEM((2 * ROWS, D), F32),
         pltpu.VMEM((2 * ROWS, D), F32),
@@ -609,9 +695,11 @@
         dma, dma((C,)),
         dma, dma((C,)),
         dma, dma((3,)),
-        dma, dma, dma((3, 2)),
+        dma, dma((3, 2)),
         dma, dma((3,)),
         dma, dma((3,)),
+        dma, dma, dma,
+        dma, dma, dma, dma, dma, dma, dma, dma, dma, dma,
         dma, dma,
         dma, dma,
         dma, dma((5,)),

time: 98.5 us -> 95.6 us (0.971)
  Pallas kernels: 97.7 us -> 94.8 us
    pallas_call x1, Pallas kernels: 94.4 us -> 91.5 us  [body(): pl.pallas_call(kernel, out_shape=(jax.ShapeDtypeStruct((ROWS, D), BF16),...]
where the time goes in v5:
time: 95.6 us; the launch traced here: 95.4 us
  Pallas kernels  94.8 us (99%)
    pallas_call x1, Pallas kernels, body(): pl.pallas_call(kernel, out_shape=(jax.ShapeDtypeStruct((ROWS, D), BF16),...  91.5 us
    pallas_call x1, Pallas kernels, body(): pl.pallas_call(place_kernel, out_shape=tuple((jax.ShapeDtypeStruct(v.shap...  3.3 us

profile of v5, /device:TPU:1, one launch (start us, length us, event | category | flops | bytes accessed | tf_op | source)
XLA Modules:
  0.0 95.4 jit_solution(10296972035457807689)
XLA Ops:
  0.6 91.5 %shard_map.110 = (bf16[512,768]{1,0:T(8,128)(2,1)}, bf16[512,768]{1,0:T(8,128)(2,1)}, f32[48,3072]{1,0:T(8,128)}, f32[192,768]{1,0:T(8,128)}, f32[1,48]{1,0:T(1,128)}) custom-call(bf16[512,768]{1,0:T(8,128)(2,1)} %bitcast.6, bf16[512,768]{1,0:T(8,128)(2,1)} %bitcast.7, s32[2,256]{1,0:T(2,128)} %idx.1, s32[2]{0:T(128)} %cnt.1, bf16[1,48]{1,0:T(2,128)(2,1)} %bitcast.10, ...), custom_call_target="tpu_custom_call" | custom-call | flops 14000000000 | bytes 10000000 | tf_op jit(solution)/shard_map/pallas_call | solution.py:709
  92.1 3.3 %shard_map.111 = (bf16[512,768]{1,0:T(8,128)(2,1)}, bf16[512,768]{1,0:T(8,128)(2,1)}, f32[48,3072]{1,0:T(8,128)}, f32[192,768]{1,0:T(8,128)}, f32[1,48]{1,0:T(1,128)}) custom-call(bf16[512,768]{1,0:T(8,128)(2,1)} %get-tuple-element.15.refs_0_, bf16[512,768]{1,0:T(8,128)(2,1)} %get-tuple-element.16.refs_1_, f32[48,3072]{1,0:T(8,128)} %get-tuple-element.17.refs_2_, ...), custom_call_target="tpu_custom_call" | custom-call | tf_op jit(solution)/shard_map/pallas_call | solution.py:727

commit v6 on v5

--- a/solution.py
+++ b/solution.py
@@ -554,6 +554,10 @@
         got(inv_s.at[0:88], a_s)
 
     def slot(t, carry):
+        @pl.when(t + 1 < C)
+        def _():
+            forward_z(t + 1)
+
         @pl.when(t + 2 < C)
         def _():
             forward_x(t + 2)
@@ -561,10 +565,6 @@
         @pl.when(t + 3 < C)
         def _():
             first_sends(t + 3)
-
-        @pl.when(t + 1 < C)
-        def _():
-            forward_z(t + 1)
 
         @pl.when(t < C)
         def _():

time: 95.6 us -> 95.2 us (level)
  no operation moved by 1% of the time
where the time goes in v6:
time: 95.2 us; the launch traced here: 95 us
  Pallas kernels  94.4 us (99%)
    pallas_call x1, Pallas kernels, body(): pl.pallas_call(kernel, out_shape=(jax.ShapeDtypeStruct((ROWS, D), BF16),...  91.1 us
    pallas_call x1, Pallas kernels, body(): pl.pallas_call(place_kernel, out_shape=tuple((jax.ShapeDtypeStruct(v.shap...  3.3 us

profile of v6, /device:TPU:1, one launch (start us, length us, event | category | flops | bytes accessed | tf_op | source)
XLA Modules:
  0.0 95.0 jit_solution(16111700048277487338)
XLA Ops:
  0.6 91.1 %shard_map.110 = (bf16[512,768]{1,0:T(8,128)(2,1)}, bf16[512,768]{1,0:T(8,128)(2,1)}, f32[48,3072]{1,0:T(8,128)}, f32[192,768]{1,0:T(8,128)}, f32[1,48]{1,0:T(1,128)}) custom-call(bf16[512,768]{1,0:T(8,128)(2,1)} %bitcast.6, bf16[512,768]{1,0:T(8,128)(2,1)} %bitcast.7, s32[2,256]{1,0:T(2,128)} %idx.1, s32[2]{0:T(128)} %cnt.1, bf16[1,48]{1,0:T(2,128)(2,1)} %bitcast.10, ...), custom_call_target="tpu_custom_call" | custom-call | flops 14000000000 | bytes 10000000 | tf_op jit(solution)/shard_map/pallas_call | solution.py:709
  91.7 3.3 %shard_map.111 = (bf16[512,768]{1,0:T(8,128)(2,1)}, bf16[512,768]{1,0:T(8,128)(2,1)}, f32[48,3072]{1,0:T(8,128)}, f32[192,768]{1,0:T(8,128)}, f32[1,48]{1,0:T(1,128)}) custom-call(bf16[512,768]{1,0:T(8,128)(2,1)} %get-tuple-element.15.refs_0_, bf16[512,768]{1,0:T(8,128)(2,1)} %get-tuple-element.16.refs_1_, f32[48,3072]{1,0:T(8,128)} %get-tuple-element.17.refs_2_, ...), custom_call_target="tpu_custom_call" | custom-call | tf_op jit(solution)/shard_map/pallas_call | solution.py:727
